TPU v7x, 256 devices: a whole 4x4x8 slice. The times are simulated.
256 devices in a mesh: replica: 32 (over y, z), tensor: 8 (over x, core).
Axes of the slice: x: 4, y: 4, z: 8, core: 2. Of those that a mesh axis runs over, the one named last changes fastest.
Arguments:
- inputs: bfloat16 [8192, 2560], P(('replica', 'tensor')), may hold values from -6 to 6
- pre_act: bfloat16 [8192, 7936], P('replica', 'tensor'), may hold values from -8 to 8
- grad_hidden: bfloat16 [8192, 7936], P('replica', 'tensor'), may hold values from -1.75 to 1.75
- up_weight: bfloat16 [2560, 7936], P('replica', 'tensor'), may hold values from -0.125 to 0.125
- error_in: bfloat16 [32, 2560, 7936], P('replica', None, 'tensor'), may hold values from -12 to 12
- q_prev: float32 [7936, 128], P('tensor'), may hold values from -0.0625 to 0.0625
Outputs:
- input_grad: bfloat16 [8192, 2560], P(('replica', 'tensor'))
- q_factor: float32 [7936, 128], P('tensor')
- error_out: bfloat16 [32, 2560, 7936], P('replica', None, 'tensor')
All inputs are finite; a program needn't handle non-finite values.
Results may differ from a plain program's by a relative error of at most 0.02.
Values may be sent and summed in bfloat16 or wider, within the bound.
No kernel may reach another device: no remote copies, remote signals or barrier semaphores. Data moves between devices by JAX's collectives and lax.ppermute only.
A program may use at most 128 MiB of HBM per device.

v0:
```python
import jax
import jax.numpy as jnp
from jax import lax
from jax.sharding import PartitionSpec as P

precise = lax.Precision.HIGHEST
root_half = 0.7071067811865476
inverse_root = 0.3989422804014327


def hidden_slope(pre_act, grad_hidden):
    values = pre_act.astype(jnp.float32)
    normal_cdf = 0.5 * (1.0 + jax.scipy.special.erf(values * root_half))
    density = jnp.exp(-0.5 * values * values) * inverse_root
    return (grad_hidden.astype(jnp.float32) * (normal_cdf + values * density)).astype(jnp.bfloat16)


def on_device(inputs, pre_act, grad_hidden, up_weight, error_in, q_prev):
    replicas = lax.axis_size("replica")
    slopes = hidden_slope(pre_act, grad_hidden)
    all_tokens = lax.all_gather(inputs, "tensor", axis=0, tiled=True)
    product = lax.dot_general(
        all_tokens, slopes, (((0,), (0,)), ((), ())), preferred_element_type=jnp.float32
    )
    combined = product + error_in[0].astype(jnp.float32)
    partial_grad = lax.dot_general(
        slopes,
        lax.all_gather(up_weight, "replica", axis=0, tiled=True),
        (((1,), (1,)), ((), ())),
        preferred_element_type=jnp.float32,
    )
    input_grad = lax.psum_scatter(partial_grad, "tensor", scatter_dimension=0, tiled=True).astype(
        jnp.bfloat16
    )
    local_basis = jnp.dot(combined, q_prev, precision=precise, preferred_element_type=jnp.float32)
    basis_sum = lax.psum(local_basis, ("replica", "tensor")) / replicas
    gram_matrix = jnp.dot(
        basis_sum.T, basis_sum, precision=precise, preferred_element_type=jnp.float32
    )
    factor = jnp.linalg.cholesky(gram_matrix)
    orthogonal = jax.scipy.linalg.solve_triangular(factor, basis_sum.T, lower=True).T
    local_factor = lax.dot_general(
        combined,
        orthogonal,
        (((0,), (0,)), ((), ())),
        precision=precise,
        preferred_element_type=jnp.float32,
    )
    q_factor = lax.psum(local_factor.astype(jnp.bfloat16), "replica").astype(jnp.float32) / replicas
    approx = jnp.dot(orthogonal, q_factor.T, precision=precise, preferred_element_type=jnp.float32)
    error_out = (combined - approx).astype(jnp.bfloat16)[None]
    return (input_grad, q_factor, error_out)


def solution(mesh):
    placed = (
        P(("replica", "tensor"), None),
        P("replica", "tensor"),
        P("replica", "tensor"),
        P("replica", "tensor"),
        P("replica", None, "tensor"),
        P("tensor", None),
    )
    return jax.shard_map(
        on_device,
        mesh=mesh,
        in_specs=placed,
        out_specs=(P(("replica", "tensor"), None), P("tensor", None), P("replica", None, "tensor")),
        check_vma=False,
    )
```

profile of v0, /device:TPU:32, one launch (start us, length us, event | category | flops | bytes accessed | tf_op | source)
XLA Modules:
  0.0 536.0 jit_solution(7953058387693800299)
XLA Ops:
  8.0 0.0 copy-start
  8.0 0.0 all-gather.5.cloned.1.call-start
  8.1 0.7 all-gather.5.cloned.1.call-update
  8.7 0.0 all-reduce.3.cloned.1.call-start
  8.8 31.1 %all-gather.5.cloned.1.call-done = bf16[256,2560]{1,0:T(8,128)(2,1)} async-done(((bf16[32,2560]{1,0:T(8,128)(2,1)}), bf16[256,2560]{1,0:T(8,128)(2,1)}) %all-gather.5.cloned.1.call-update) | async-done | bytes 1310736 | tf_op jit(solution)/shard_map/all_gather | solution.py:21
  39.9 5.0 convert_add_fusion
  44.9 3.9 copy-done.1
  48.8 18.0 %fusion.23 = f32[2560,128]{1,0:T(8,128)} fusion(f32[2560,992]{0,1:T(8,128)S(1)} %convert_add_fusion, f32[992,128]{1,0:T(8,128)S(1)} %copy-done), kind=kOutput, calls=%fused_computation.35 | convolution fusion | flops 3900702720 | bytes 11976704 | tf_op jit(solution)/shard_map/dot_general | solution.py:35
  66.8 0.0 all-reduce.3.cloned.1.call-update
  66.8 0.0 all-gather.3.cloned.1.call-start
  66.8 0.5 all-gather.3.cloned.1.call-update
  67.4 0.2 all-reduce.5.cloned.1.call-start
  67.6 261.9 %all-reduce.3.cloned.1.call-done = f32[2560,128]{1,0:T(8,128)} async-done(((f32[2560,128]{1,0:T(8,128)}), f32[2560,128]{1,0:T(8,128)}) %all-reduce.3.cloned.1.call-update) | async-done | bytes 1310736 | tf_op jit(solution)/shard_map/psum | solution.py:36
  329.5 4.1 fusion.3
  333.6 0.1 copy.9
  333.7 11.7 %cholesky.16 = f32[128,128]{1,0:T(8,128)S(1)} custom-call(f32[128,128]{1,0:T(8,128)S(1)} %fusion.17), custom_call_target="Cholesky" | custom-call | tf_op jit(solution)/shard_map/jit(cholesky)/cholesky | solution.py:40
  345.4 0.6 compare_reduce_fusion
  346.1 0.7 fusion.15
  346.8 9.8 %custom-call.7 = f32[1,128,128]{1,2,0:T(8,128)S(1)} custom-call(f32[1,128,128]{2,1,0:T(8,128)S(1)} %fusion.15), custom_call_target="InvertDiagBlocksLowerTriangular" | custom-call | tf_op jit(solution)/shard_map/jit(_solve_triangular)/triangular_solve | solution.py:41
  356.6 1.3 fusion.1
  357.9 0.0 copy-start.4
  357.9 11.6 %convolution_convert_fusion = bf16[992,128]{1,0:T(8,128)(2,1)} fusion(f32[2560,992]{0,1:T(8,128)} %copy-done.1, f32[128,2560]{1,0:T(8,128)S(1)} %fusion.1), kind=kOutput, calls=%fused_computation.11 | convolution fusion | flops 3900829696 | bytes 11722752 | tf_op jit(solution)/shard_map/dot_general | solution.py:42
  369.5 0.0 all-reduce.5.cloned.1.call-update
  369.5 0.0 reduce-scatter.2.cloned.1.call-start
  369.6 0.0 all-gather.3.cloned.1.call-done
  369.6 5.9 %fusion.21 = f32[256,2560]{1,0:T(8,128)} fusion(bf16[2560,992]{1,0:T(8,128)(2,1)} %all-gather.3.cloned.1.call-done, bf16[256,992]{0,1:T(8,128)(2,1)S(1)} %copy-done.4, bf16[256,992]{0,1:T(8,128)(2,1)S(1)} %copy-done.5), kind=kOutput, calls=%fused_computation.34 | convolution fusion | flops 1303281664 | bytes 8716288 | tf_op jit(solution)/shard_map/dot_general | solution.py:26
  375.5 0.0 reduce-scatter.2.cloned.1.call-update
  375.6 138.0 %all-reduce.5.cloned.1.call-done = bf16[992,128]{1,0:T(8,128)(2,1)} async-done(((bf16[992,128]{1,0:T(8,128)(2,1)}), bf16[992,128]{1,0:T(8,128)(2,1)}) %all-reduce.5.cloned.1.call-update) | async-done | bytes 253968 | tf_op jit(solution)/shard_map/psum | solution.py:49
  513.5 1.0 convert_multiply_fusion.4
  514.5 0.0 copy-start.3
  514.5 12.4 %fusion = bf16[1,2560,992]{1,2,0:T(8,128)(2,1)} fusion(f32[2560,992]{0,1:T(8,128)} %copy-done.1, f32[128,2560]{1,0:T(8,128)S(1)} %fusion.1, f32[992,128]{1,0:T(8,128)S(1)} %convert_multiply_fusion.4), kind=kOutput, calls=%fused_computation.2 | convolution fusion | flops 3905781760 | bytes 17055744 | tf_op jit(solution)/shard_map/dot_general | solution.py:50
  527.0 1.7 convert_element_type.30
  (11 shorter events, 0.1 us)
Async XLA Ops:
  8.0 40.8 %copy-start = (f32[992,128]{1,0:T(8,128)S(1)}, f32[992,128]{1,0:T(8,128)}, u32[]{:S(2)}) copy-start(f32[992,128]{1,0:T(8,128)} %param.11) | copy-start | bytes 1523716
  8.0 31.9 %all-gather.5.cloned.1.call-start = ((), (), s32[]{:S(2)}) async-start(), calls=%async_computation.3 | async-start | bytes 1474560 | tf_op jit(solution)/shard_map/all_gather | solution.py:21
  8.7 320.7 %all-reduce.3.cloned.1.call-start = ((), (), s32[]{:S(2)}) async-start(), calls=%async_computation.4 | async-start | bytes 2621440 | tf_op jit(solution)/shard_map/psum | solution.py:36
  44.9 3.9 copy-start.1
  66.8 302.8 %all-gather.3.cloned.1.call-start = ((), (), s32[]{:S(2)}) async-start(), calls=%async_computation.1 | async-start | bytes 5406720 | tf_op jit(solution)/shard_map/all_gather | solution.py:28
  67.4 446.2 %all-reduce.5.cloned.1.call-start = ((), (), s32[]{:S(2)}) async-start(), calls=%async_computation.5 | async-start | bytes 507904 | tf_op jit(solution)/shard_map/psum | solution.py:49
  329.5 27.1 %copy-start.2 = (f32[2560,128]{1,0:T(8,128)S(1)}, f32[2560,128]{1,0:T(8,128)}, u32[]{:S(2)}) copy-start(f32[2560,128]{1,0:T(8,128)} %all-reduce.3.cloned.1.call-done) | copy-start | bytes 3932164
  357.9 11.7 %copy-start.4 = (bf16[256,992]{0,1:T(8,128)(2,1)S(1)}, bf16[256,992]{0,1:T(8,128)(2,1)}, u32[]{:S(2)}) copy-start(bf16[256,992]{0,1:T(8,128)(2,1)} %param.7) | copy-start | bytes 1523716
  357.9 11.7 %copy-start.5 = (bf16[256,992]{0,1:T(8,128)(2,1)S(1)}, bf16[256,992]{0,1:T(8,128)(2,1)}, u32[]{:S(2)}) copy-start(bf16[256,992]{0,1:T(8,128)(2,1)} %param.8) | copy-start | bytes 1523716
  369.5 157.5 %reduce-scatter.2.cloned.1.call-start = ((), (), s32[]{:S(2)}) async-start(), calls=%async_computation.2 | async-start | bytes 2949120 | tf_op jit(solution)/shard_map/reduce_scatter | solution.py:32
  514.5 12.5 %copy-start.3 = (f32[992,128]{1,0:T(8,128)}, f32[992,128]{1,0:T(8,128)S(1)}, u32[]{:S(2)}) copy-start(f32[992,128]{1,0:T(8,128)S(1)} %convert_multiply_fusion.4) | copy-start | bytes 1523716
Sparse Core Ops, SparseCore 0:
  10.7 29.1 all-gather.4
  66.9 262.5 all-reduce.2
  375.7 38.1 reduce-scatter.1
Sparse Core Ops, SparseCore 1:
  70.2 85.2 all-gather.2
  369.6 143.9 all-reduce.4
where the time goes:
time: 546 us; the launch traced here: 536 us
  waiting for transfers between devices  432 us (79%)
  matrix products  58.3 us (11%)
  other arithmetic  25.5 us (5%)
  between operations  15.5 us (3%)
    psum x1, waiting for transfers between devices, on_device(): basis_sum = lax.psum(local_basis, ('replica', 'tensor')) / replicas  262 us
    psum x1, waiting for transfers between devices, on_device(): lax.psum(local_factor.astype(jnp.bfloat16), 'replica').astype(jnp.float32)  138 us
    all_gather x1, waiting for transfers between devices, on_device(): all_tokens = lax.all_gather(inputs, 'tensor', axis=0, tiled=True)  31.1 us
    dot_general x1, matrix products, on_device(): jnp.dot(combined, q_prev, precision=precise, preferred_element_type=jnp.f...  18 us
    dot_general x1, matrix products, on_device(): jnp.dot(orthogonal, q_factor.T, precision=precise, preferred_element_type...  12.4 us
    another operation x3, other arithmetic, on_device(): factor = jnp.linalg.cholesky(gram_matrix)  12.4 us
    dot_general x1, matrix products, on_device(): lax.dot_general(combined, orthogonal, (((0,), (0,)), ((), ())), precision...  11.6 us
  transfers between devices with their start and end apart: 5, of which 3 were waited for; matrix products, arithmetic and copies ran while one was open for 11% of the time, Pallas kernels for 0%

commit v1 on v0

v1 whole, which is shorter than its diff:
```python
import jax
import jax.numpy as jnp
from jax import lax
from jax.sharding import PartitionSpec as P

f32, bf16 = jnp.float32, jnp.bfloat16
precise = lax.Precision.HIGHEST
root_half = 0.7071067811865476
inverse_root = 0.3989422804014327

RANK = 128
CORE_PAIRS = [(i, i ^ 1) for i in range(8)]
CHIP_GROUPS = [[core + 2 * chip for chip in range(4)] for core in range(2)]


def hidden_slope(pre_act, grad_hidden):
    values = pre_act.astype(f32)
    normal_cdf = 0.5 * (1.0 + jax.scipy.special.erf(values * root_half))
    density = jnp.exp(-0.5 * values * values) * inverse_root
    return (grad_hidden.astype(f32) * (normal_cdf + values * density)).astype(bf16)


def split(values):
    high = lax.reduce_precision(values, 8, 7)
    return high.astype(bf16), (values - high).astype(bf16)


def dot(left, right, left_dim, right_dim):
    return lax.dot_general(
        left, right, (((left_dim,), (right_dim,)), ((), ())), preferred_element_type=f32
    )


def dot_pair(left, right, left_dim):
    both = dot(left, jnp.concatenate(split(right), axis=1), left_dim, 0)
    return both[:, :RANK] + both[:, RANK:]


def reduce_tensor(values):
    core = lax.axis_index("tensor") % 2
    half = values.shape[0] // 2
    halves = values.reshape(2, half, RANK)
    kept = lax.dynamic_index_in_dim(halves, core, 0, keepdims=False)
    sent = lax.dynamic_index_in_dim(halves, 1 - core, 0, keepdims=False)
    kept = kept + lax.ppermute(sent, "tensor", CORE_PAIRS)
    blocks = lax.all_to_all(
        kept.reshape(4, half // 4, RANK), "tensor", 0, 0, axis_index_groups=CHIP_GROUPS
    )
    return jnp.sum(blocks, axis=0)


def gather_tensor(rows):
    blocks = lax.all_to_all(
        jnp.broadcast_to(rows[None], (4, *rows.shape)),
        "tensor",
        0,
        0,
        axis_index_groups=CHIP_GROUPS,
    )
    mine = blocks.reshape(-1, RANK)
    other = lax.ppermute(mine, "tensor", CORE_PAIRS)
    first = lax.axis_index("tensor") % 2 == 0
    return jnp.concatenate([jnp.where(first, mine, other), jnp.where(first, other, mine)], axis=0)


def reduce_replica(values, rows):
    padded = jnp.pad(values, ((0, 32 * rows - values.shape[0]), (0, 0))).reshape(32, rows, RANK)
    return jnp.sum(lax.all_to_all(padded, "replica", 0, 0).astype(f32), axis=0)


def gather_replica(block, count):
    blocks = lax.all_to_all(jnp.broadcast_to(block[None], (32, *block.shape)), "replica", 0, 0)
    return blocks.reshape(-1, RANK)[:count]


def on_device(inputs, pre_act, grad_hidden, up_weight, error_in, q_prev):
    replicas = lax.axis_size("replica")
    error = error_in[0]
    weights = lax.all_gather(up_weight, "replica", axis=0, tiled=True)
    tokens = lax.all_gather(inputs, "tensor", axis=0, tiled=True)
    slopes = hidden_slope(pre_act, grad_hidden)
    with jax.named_scope("basis"):
        slope_terms = dot_pair(slopes, q_prev, 1)
        own_slopes = jnp.sum(
            lax.all_to_all(slope_terms.reshape(8, -1, RANK), "tensor", 0, 0), axis=0
        )
        basis_terms = dot_pair(error, q_prev, 1) + dot_pair(inputs, own_slopes, 0)
        rows = reduce_tensor(basis_terms)
        rows = reduce_replica(rows, 16) / replicas
        basis_sum = gather_tensor(gather_replica(rows, 320))
    with jax.named_scope("orthonormal"):
        gram_matrix = jnp.dot(basis_sum.T, basis_sum, precision=precise, preferred_element_type=f32)
        factor = jnp.linalg.cholesky(gram_matrix)
        orthogonal = jax.scipy.linalg.solve_triangular(factor, basis_sum.T, lower=True).T
    with jax.named_scope("right_factor"):
        local_factor = dot_pair(error, orthogonal, 0) + dot_pair(
            slopes, dot_pair(tokens, orthogonal, 1), 0
        )
        block = reduce_replica(local_factor.astype(bf16), 32) / replicas
        q_factor = gather_replica(block.astype(bf16), 992).astype(f32)
    with jax.named_scope("residual"):
        p_high, p_low = split(orthogonal)
        q_high = q_factor.astype(bf16)
        approx = dot(
            jnp.concatenate([p_high, p_low], axis=1),
            jnp.concatenate([q_high, q_high], axis=1),
            1,
            1,
        )
        error_out = (dot(tokens, slopes, 0, 0) + error.astype(f32) - approx).astype(bf16)[None]
    with jax.named_scope("input_grad"):
        partial_grad = dot(slopes, weights, 1, 1)
        input_grad = lax.psum_scatter(
            partial_grad, "tensor", scatter_dimension=0, tiled=True
        ).astype(bf16)
    return (input_grad, q_factor, error_out)


def solution(mesh):
    placed = (
        P(("replica", "tensor"), None),
        P("replica", "tensor"),
        P("replica", "tensor"),
        P("replica", "tensor"),
        P("replica", None, "tensor"),
        P("tensor", None),
    )
    return jax.shard_map(
        on_device,
        mesh=mesh,
        in_specs=placed,
        out_specs=(P(("replica", "tensor"), None), P("tensor", None), P("replica", None, "tensor")),
        check_vma=False,
    )
```

time: 546 us -> 193 us (0.35); the launches traced: 536 us -> 192 us
  waiting for transfers between devices: 432 us -> 24.9 us
  blocking collectives: 0 us -> 61.9 us
  matrix products: 58.3 us -> 34.3 us
  starting transfers between devices: 0.37 us -> 20.3 us
    psum x2 -> x0, waiting for transfers between devices: 400 us -> none  [the longest x1 262 us: on_device(): basis_sum = lax.psum(local_basis, ('replica', 'tensor')) / replicas]
    all_to_all x0 -> x4, blocking collectives: none -> 61.9 us  [the longest x1 18.2 us: gather_replica(): lax.all_to_all(jnp.broadcast_to(block[None], (32, *block.shape)), 'replic...]
    all_gather x2, waiting for transfers between devices: 31.1 us -> 3.26 us  [the longest x1 3.24 us: on_device(): weights = lax.all_gather(up_weight, 'replica', axis=0, tiled=True)]
    dot_general x5 -> x9, matrix products: 52.9 us -> 30.8 us  [dot(): lax.dot_general(left, right, (((left_dim,), (right_dim,)), ((), ())), pre...]
    all_to_all x0 -> x3, starting transfers between devices: none -> 20 us  [the longest x1 11.4 us: reduce_replica(): return jnp.sum(lax.all_to_all(padded, 'replica', 0, 0).astype(f32), axis=0)]
    all_to_all x0 -> x3, waiting for transfers between devices: none -> 18.7 us  [the longest x1 10.9 us: reduce_replica(): return jnp.sum(lax.all_to_all(padded, 'replica', 0, 0).astype(f32), axis=0)]
  transfers between devices with their start and end apart: 5 -> 8, of which waited for: 3 -> 5; matrix products, arithmetic and copies ran while one was open for 11% -> 36% of each run, Pallas kernels for 0% -> 0%
where the time goes in v1:
time: 193 us; the launch traced here: 192 us
  blocking collectives  61.9 us (32%)
  matrix products  34.3 us (18%)
  other arithmetic  30.5 us (16%)
  waiting for transfers between devices  24.9 us (13%)
  starting transfers between devices  20.3 us (11%)
  between operations  14.1 us (7%)
  local copies, waits for them, and re-layouts  5.91 us (3%)
    dot_general x9, matrix products, dot(): lax.dot_general(left, right, (((left_dim,), (right_dim,)), ((), ())), pre...  30.8 us
    all_to_all x1, blocking collectives, gather_replica(): lax.all_to_all(jnp.broadcast_to(block[None], (32, *block.shape)), 'replic...  18.2 us
    all_to_all x1, blocking collectives, reduce_replica(): return jnp.sum(lax.all_to_all(padded, 'replica', 0, 0).astype(f32), axis=0)  17.9 us
    all_to_all x1, blocking collectives, reduce_tensor(): lax.all_to_all(kept.reshape(4, half // 4, RANK), 'tensor', 0, 0, axis_ind...  13.9 us
    another operation x3, other arithmetic, on_device(): factor = jnp.linalg.cholesky(gram_matrix)  12.4 us
    all_to_all x1, blocking collectives, gather_tensor(): lax.all_to_all(jnp.broadcast_to(rows[None], (4, *rows.shape)), 'tensor',...  11.9 us
    all_to_all x1, starting transfers between devices, reduce_replica(): return jnp.sum(lax.all_to_all(padded, 'replica', 0, 0).astype(f32), axis=0)  11.4 us
    all_to_all x1, waiting for transfers between devices, reduce_replica(): return jnp.sum(lax.all_to_all(padded, 'replica', 0, 0).astype(f32), axis=0)  10.9 us
  transfers between devices with their start and end apart: 8, of which 5 were waited for; matrix products, arithmetic and copies ran while one was open for 36% of the time, Pallas kernels for 0%

profile of v1, /device:TPU:32, one launch (start us, length us, event | category | flops | bytes accessed | tf_op | source)
XLA Modules:
  0.0 191.9 jit_solution(16428893883964186338)
XLA Ops:
  7.9 1.1 reduce-precision_convert_fusion.1
  10.6 4.3 %all-to-all-start = ((f32[8,32,128]{2,1,0:T(8,128)}), f32[8,32,128]{2,1,0:T(8,128)}, u32[]{:S(2)}, u32[]{:S(2)}) async-start(f32[8,32,128]{2,1,0:T(8,128)} %bitcast.2), calls=%async_computation.1 | async-start | bytes 262144 | tf_op jit(solution)/shard_map/basis/all_to_all | solution.py:85
  14.9 4.2 %fusion.7 = f32[2560,256]{0,1:T(8,128)S(1)} fusion(bf16[1,2560,992]{1,2,0:T(8,128)(2,1)} %param.10, bf16[992,128]{1,0:T(8,128)(2,1)} %copy-done.1, bf16[992,128]{1,0:T(8,128)(2,1)S(1)} %get-tuple-element.9), kind=kOutput, calls=%fused_computation.8 | convolution fusion | flops 1301250048 | bytes 8208384 | tf_op jit(solution)/shard_map/basis/dot_general | solution.py:29
  19.1 2.0 %all-to-all-done = f32[8,32,128]{2,1,0:T(8,128)} async-done(((f32[8,32,128]{2,1,0:T(8,128)}), f32[8,32,128]{2,1,0:T(8,128)}, u32[]{:S(2)}, u32[]{:S(2)}) %all-to-all-start) | async-done | bytes 131104 | tf_op jit(solution)/shard_map/basis/all_to_all | solution.py:85
  21.1 0.9 reduce_sum.36
  22.6 1.5 fusion.14
  24.1 2.2 %reshape.48 = f32[2,1280,128]{1,0,2:T(2,128)S(1)} reshape(f32[2560,128]{0,1:T(8,128)} %fusion.14) | data formatting | bytes 2621440 | tf_op jit(solution)/shard_map/basis/reshape | solution.py:42
  26.3 1.1 constant_dynamic-slice_fusion.1
  28.5 1.6 collective-permute-done
  30.1 13.9 %all_to_all.35 = f32[4,320,128]{2,1,0:T(8,128)S(1)} all-to-all(f32[4,320,128]{2,1,0:T(8,128)S(1)} %bitcast.65), channel_id=1, replica_groups={{0,2,4,6},{1,3,5,7},{8,10,12,14},{9,11,13,15},{16,18,20,22},{17,19,21,2..., dimensions={0} | all-to-all | bytes 1310720 | tf_op jit(solution)/shard_map/basis/all_to_all | solution.py:46
  44.1 0.7 pad.8
  44.8 11.4 %all-to-all-start.2 = ((f32[32,16,128]{2,1,0:T(8,128)}), f32[32,16,128]{2,1,0:T(8,128)S(1)}, u32[]{:S(2)}, u32[]{:S(2)}) async-start(f32[32,16,128]{2,1,0:T(8,128)} %bitcast.7), calls=%async_computation.3 | async-start | bytes 524288 | tf_op jit(solution)/shard_map/basis/all_to_all | solution.py:68
  56.2 0.7 all-gather.5.cloned.1.call-update
  56.9 10.9 %all-to-all-done.2 = f32[32,16,128]{2,1,0:T(8,128)S(1)} async-done(((f32[32,16,128]{2,1,0:T(8,128)}), f32[32,16,128]{2,1,0:T(8,128)S(1)}, u32[]{:S(2)}, u32[]{:S(2)}) %all-to-all-start.2) | async-done | bytes 262176 | tf_op jit(solution)/shard_map/basis/all_to_all | solution.py:68
  68.0 18.2 %all_to_all.36 = f32[32,16,128]{2,1,0:T(8,128)S(1)} all-to-all(f32[32,16,128]{2,1,0:T(8,128)S(1)} %broadcast_in_dim.12), channel_id=1, replica_groups=mesh['replica'=32,'tensor'=8] {'replica'}, dimensions={0} | all-to-all | bytes 524288 | tf_op jit(solution)/shard_map/basis/all_to_all | solution.py:72
  86.2 11.9 %all_to_all.37 = f32[4,320,128]{2,1,0:T(8,128)S(1)} all-to-all(f32[4,320,128]{2,1,0:T(8,128)S(1)} %broadcast_in_dim.14), channel_id=1, replica_groups={{0,2,4,6},{1,3,5,7},{8,10,12,14},{9,11,13,15},{16,18,20,22},{17,19,21,2..., dimensions={0} | all-to-all | bytes 1310720 | tf_op jit(solution)/shard_map/basis/all_to_all | solution.py:53
  98.1 3.2 %all-gather.3.cloned.1.call-done = bf16[2560,992]{1,0:T(8,128)(2,1)} async-done(((bf16[80,992]{1,0:T(8,128)(2,1)}), bf16[2560,992]{1,0:T(8,128)(2,1)}) %all-gather.3.cloned.1.call-update) | async-done | bytes 5079056 | tf_op jit(solution)/shard_map/all_gather | solution.py:79
  101.4 5.6 %fusion.53 = f32[256,2560]{1,0:T(8,128)} fusion(bf16[256,992]{0,1:T(8,128)(2,1)S(1)} %fusion.24, bf16[2560,992]{1,0:T(8,128)(2,1)} %all-gather.3.cloned.1.call-done), kind=kOutput, calls=%fused_computation.88 | convolution fusion | flops 1300234240 | bytes 8208384 | tf_op jit(solution)/shard_map/input_grad/dot_general | solution.py:29
  107.1 2.2 %fusion.16 = f32[128,128]{1,0:T(8,128)S(1)} fusion(f32[1280,128]{1,0:T(8,128)S(1)} %get-tuple-element.6, f32[1280,128]{1,0:T(8,128)S(1)} %get-tuple-element.5), kind=kOutput, calls=%fused_computation.25 | convolution fusion | flops 503644160 | bytes 1376256 | tf_op jit(solution)/shard_map/orthonormal/dot_general | solution.py:92
  109.4 11.7 %cholesky.16 = f32[128,128]{1,0:T(8,128)S(1)} custom-call(f32[128,128]{1,0:T(8,128)S(1)} %fusion.39), custom_call_target="Cholesky" | custom-call | tf_op jit(solution)/shard_map/orthonormal/jit(cholesky)/cholesky | solution.py:93
  122.5 9.8 %custom-call.7 = f32[1,128,128]{1,2,0:T(8,128)S(1)} custom-call(f32[1,128,128]{2,1,0:T(8,128)S(1)} %fusion.37), custom_call_target="InvertDiagBlocksLowerTriangular" | custom-call | tf_op jit(solution)/shard_map/orthonormal/jit(_solve_triangular)/triangular_solve | solution.py:94
  132.3 1.4 reduce-precision_convert_fusion
  133.7 1.9 convolution_bitcast_fusion.1
  135.9 4.2 %fusion.10 = f32[992,256]{1,0:T(8,128)S(1)} fusion(bf16[1,2560,992]{1,2,0:T(8,128)(2,1)} %param.10, bf16[2560,128]{0,1:T(8,128)(2,1)S(1)} %get-tuple-element.4, bf16[2560,128]{0,1:T(8,128)(2,1)S(1)} %get-tuple-element.3), kind=kOutput, calls=%fused_computation.16 | convolution fusion | flops 1302855680 | bytes 7405568 | tf_op jit(solution)/shard_map/right_factor/dot_general | solution.py:29
  140.2 17.9 %all_to_all.38 = bf16[32,32,128]{2,1,0:T(8,128)(2,1)S(1)} all-to-all(bf16[32,32,128]{2,1,0:T(8,128)(2,1)S(1)} %bitcast.67), channel_id=1, replica_groups=mesh['replica'=32,'tensor'=8] {'replica'}, dimensions={0} | all-to-all | bytes 524288 | tf_op jit(solution)/shard_map/right_factor/all_to_all | solution.py:68
  158.2 0.7 broadcast_in_dim.28
  158.9 4.4 %all-to-all-start.6 = ((bf16[32,32,128]{2,1,0:T(8,128)(2,1)}), bf16[32,32,128]{2,1,0:T(8,128)(2,1)S(1)}, u32[]{:S(2)}, u32[]{:S(2)}) async-start(bf16[32,32,128]{2,1,0:T(8,128)(2,1)} %broadcast_in_dim.28), calls=%async_computation.7 | async-start | bytes 524288 | tf_op jit(solution)/shard_map/right_factor/all_to_all | solution.py:72
  163.3 5.4 %fusion.54 = f32[992,2560]{1,0:T(8,128)} fusion(bf16[256,992]{0,1:T(8,128)(2,1)S(1)} %fusion.24, bf16[256,2560]{1,0:T(8,128)(2,1)S(1)} %copy-done), kind=kOutput, calls=%fused_computation.89 | convolution fusion | flops 1300234240 | bytes 11976704 | tf_op jit(solution)/shard_map/residual/dot_general | solution.py:29
  168.7 5.7 %all-to-all-done.6 = bf16[32,32,128]{2,1,0:T(8,128)(2,1)S(1)} async-done(((bf16[32,32,128]{2,1,0:T(8,128)(2,1)}), bf16[32,32,128]{2,1,0:T(8,128)(2,1)S(1)}, u32[]{:S(2)}, u32[]{:S(2)}) %all-to-all-start.6) | async-done | bytes 262176 | tf_op jit(solution)/shard_map/right_factor/all_to_all | solution.py:72
  174.4 0.8 bitcast_convert_fusion
  175.2 8.5 %fusion.6 = bf16[1,2560,992]{1,2,0:T(8,128)(2,1)} fusion(bf16[1,2560,992]{1,2,0:T(8,128)(2,1)} %param.10, f32[992,2560]{1,0:T(8,128)} %fusion.54, bf16[992,128]{1,0:T(8,128)(2,1)S(1)} %bitcast.66, bf16[2560,128]{0,1:T(8,128)(2,1)S(1)} %get-tuple-element.4, bf16[2560,128]{0,1:T(8,128)(2,1)S(1)} %get-tuple-element.3), kind=kOutput, calls=%fused_computation.7 | convolution fusion | flops 1314029568 | bytes 21880832 | tf_op jit(solution)/shard_map/residual/dot_general | solution.py:29
  183.7 1.7 convert_element_type.72
  (47 shorter events, 6.2 us)
Async XLA Ops:
  7.2 1.9 copy-start.3
  7.2 1.9 copy-start.4
  7.2 94.2 %all-gather.3.cloned.1.call-start = ((), (), s32[]{:S(2)}) async-start(), calls=%async_computation.8 | async-start | bytes 5406720 | tf_op jit(solution)/shard_map/all_gather | solution.py:79
  9.1 0.9 copy-start.1
  10.6 10.5 %all-to-all-start = ((f32[8,32,128]{2,1,0:T(8,128)}), f32[8,32,128]{2,1,0:T(8,128)}, u32[]{:S(2)}, u32[]{:S(2)}) async-start(f32[8,32,128]{2,1,0:T(8,128)} %bitcast.2), calls=%async_computation.1 | async-start | bytes 262144 | tf_op jit(solution)/shard_map/basis/all_to_all | solution.py:85
  14.9 7.2 %copy-start.2 = (bf16[32,2560]{1,0:T(8,128)(2,1)S(1)}, bf16[32,2560]{1,0:T(8,128)(2,1)}, u32[]{:S(2)}) copy-start(bf16[32,2560]{1,0:T(8,128)(2,1)} %param.6) | copy-start | bytes 491524
  27.9 2.2 %collective-permute-start = (f32[1280,128]{1,0:T(8,128)S(1)}, f32[1280,128]{1,0:T(8,128)S(1)}, u32[]{:S(2)}, u32[]{:S(2)}) collective-permute-start(f32[1280,128]{1,0:T(8,128)S(1)} %bitcast.68), channel_id=1, source_target_pairs={{0,1},{1,0},{2,3},{3,2},{4,5},{5,4},{6,7},{7,6},{8,9},{9,8},{10,11... | collective-permute-start | bytes 1966088 | tf_op jit(solution)/shard_map/basis/ppermute | solution.py:45
  44.8 23.1 %all-to-all-start.2 = ((f32[32,16,128]{2,1,0:T(8,128)}), f32[32,16,128]{2,1,0:T(8,128)S(1)}, u32[]{:S(2)}, u32[]{:S(2)}) async-start(f32[32,16,128]{2,1,0:T(8,128)} %bitcast.7), calls=%async_computation.3 | async-start | bytes 524288 | tf_op jit(solution)/shard_map/basis/all_to_all | solution.py:68
  56.1 77.5 %all-gather.5.cloned.1.call-start = ((), (), s32[]{:S(2)}) async-start(), calls=%async_computation.10 | async-start | bytes 1474560 | tf_op jit(solution)/shard_map/all_gather | solution.py:80
  56.9 126.8 %reduce-scatter.2.cloned.1.call-start = ((), (), s32[]{:S(2)}) async-start(), calls=%async_computation.9 | async-start | bytes 2949120 | tf_op jit(solution)/shard_map/input_grad/reduce_scatter | solution.py:113
  98.1 8.8 %collective-permute-start.1 = (f32[1280,128]{1,0:T(8,128)S(1)}, f32[1280,128]{1,0:T(8,128)S(1)}, u32[]{:S(2)}, u32[]{:S(2)}) collective-permute-start(f32[1280,128]{1,0:T(8,128)S(1)} %bitcast.64), channel_id=1, source_target_pairs={{0,1},{1,0},{2,3},{3,2},{4,5},{5,4},{6,7},{7,6},{8,9},{9,8},{10,11... | collective-permute-start | bytes 1966088 | tf_op jit(solution)/shard_map/basis/ppermute | solution.py:61
  140.2 23.1 %copy-start = (bf16[256,2560]{1,0:T(8,128)(2,1)S(1)}, bf16[256,2560]{1,0:T(8,128)(2,1)}, u32[]{:S(2)}) copy-start(bf16[256,2560]{1,0:T(8,128)(2,1)} %all-gather.5.cloned.1.call-done) | copy-start | bytes 3932164
  158.9 15.4 %all-to-all-start.6 = ((bf16[32,32,128]{2,1,0:T(8,128)(2,1)}), bf16[32,32,128]{2,1,0:T(8,128)(2,1)S(1)}, u32[]{:S(2)}, u32[]{:S(2)}) async-start(bf16[32,32,128]{2,1,0:T(8,128)(2,1)} %broadcast_in_dim.28), calls=%async_computation.7 | async-start | bytes 524288 | tf_op jit(solution)/shard_map/right_factor/all_to_all | solution.py:72
Sparse Core Ops, SparseCore 0:
  10.6 90.7 all-gather.2
  103.2 24.2 all-gather.4
  130.1 37.3 reduce-scatter.1

commit v2 on v0

v2 whole, which is shorter than its diff:
```python
import jax
import jax.numpy as jnp
from jax import lax
from jax.experimental import pallas as pl
from jax.experimental.pallas import tpu as pltpu
from jax.sharding import PartitionSpec as P

f32, bf16 = jnp.float32, jnp.bfloat16
precise = lax.Precision.HIGHEST
root_half = 0.7071067811865476
inverse_root = 0.3989422804014327

RANK = 128
DW = 2560
HALF = DW // 2
HIDDEN = 992
TILE = 256
CORE_PAIRS = [(i, i ^ 1) for i in range(8)]
X_GROUPS = [[core + 2 * x for x in range(4)] for core in range(2)]
XY_GROUPS = [
    [((y * 8 + z) * 4 + x) * 2 + core for y in range(4) for x in range(4)]
    for z in range(8)
    for core in range(2)
]
Z_GROUPS = [[y * 8 + z for z in range(8)] for y in range(4)]
BOTH = ("replica", "tensor")


def hidden_slope(pre_act, grad_hidden):
    values = pre_act.astype(f32)
    normal_cdf = 0.5 * (1.0 + jax.scipy.special.erf(values * root_half))
    density = jnp.exp(-0.5 * values * values) * inverse_root
    return (grad_hidden.astype(f32) * (normal_cdf + values * density)).astype(bf16)


def dot(left, right, left_dim, right_dim, precision=None):
    return lax.dot_general(
        left,
        right,
        (((left_dim,), (right_dim,)), ((), ())),
        precision=precision,
        preferred_element_type=f32,
    )


def split_outside(values):
    high = lax.reduce_precision(values, 8, 7)
    return jnp.concatenate([high.astype(bf16), (values - high).astype(bf16)], axis=1)


def split(values):
    high = values.astype(bf16)
    return jnp.concatenate([high, (values - high.astype(f32)).astype(bf16)], axis=1)


def folded(both):
    return both[:, :RANK] + both[:, RANK:]


def broadcast_exchange(block, count, axis, groups=None):
    blocks = jnp.broadcast_to(block[None], (count, *block.shape))
    return lax.all_to_all(blocks, axis, 0, 0, axis_index_groups=groups)


def whole(shape, memory=pltpu.VMEM):
    return pl.BlockSpec(shape, lambda *_: (0,) * len(shape), memory_space=memory)


def terms_kernel(core_ref, mine_ref, other_ref, z_ref, error_ref, kept_ref, sent_ref, tokens_ref):
    core = core_ref[0]
    for x in range(4):
        for ref, owner in ((mine_ref, core), (other_ref, 1 - core)):
            start = pl.multiple_of((2 * x + owner) * 32, 32)
            tokens_ref[pl.ds(start, 32), :] = ref[x]
    both = split(z_ref[...])
    for ref, part in ((kept_ref, core), (sent_ref, 1 - core)):
        start = pl.multiple_of(part * HALF, HALF)
        columns = tokens_ref[:, pl.ds(start, HALF)]
        ref[...] = folded(dot(columns, both, 0, 0)) + error_ref[pl.ds(start, HALF), :]


def left_terms(core, mine, other, slope_terms, error_terms):
    return pl.pallas_call(
        terms_kernel,
        out_shape=(
            jax.ShapeDtypeStruct((HALF, RANK), f32),
            jax.ShapeDtypeStruct((HALF, RANK), f32),
            jax.ShapeDtypeStruct((256, DW), bf16),
        ),
        in_specs=[pl.BlockSpec(memory_space=pltpu.SMEM)]
        + [pl.BlockSpec(memory_space=pltpu.VMEM)] * 4,
        out_specs=[pl.BlockSpec(memory_space=pltpu.VMEM)] * 3,
        compiler_params=pltpu.CompilerParams(vmem_limit_bytes=32 * 2**20),
        cost_estimate=pl.CostEstimate(
            flops=2 * 256 * DW * 256, bytes_accessed=6_000_000, transcendentals=0
        ),
        name="left_terms",
    )(core, mine, other, slope_terms, error_terms)


def invert_factor(gram, work_ref, out_ref):
    sub = lax.broadcasted_iota(jnp.int32, (8, RANK), 0)
    lane = lax.broadcasted_iota(jnp.int32, (8, RANK), 1)
    work_ref[...] = gram

    def spread(rows, column):
        return jnp.broadcast_to(rows[:, column : column + 1], (8, RANK))

    def row(values, k):
        return jnp.broadcast_to(values[k : k + 1, :], (8, RANK))

    current = work_ref[0:8, :]
    for r in range(16):
        base = 8 * r
        last = r == 15
        inside = (lane >= base) & (lane < base + 8)
        columns = [spread(current, base + k) for k in range(8)]
        current = jnp.where(inside, jnp.where(lane - base == sub, 1.0, 0.0), current)
        if not last:
            after = work_ref[base + 8 : base + 16, :]
            after_columns = [spread(after, base + k) for k in range(8)]
            after = jnp.where(inside, 0.0, after)
        inverse = jnp.zeros((8, RANK), f32)
        for k in range(8):
            pivot_inverse = 1.0 / row(columns[k], k)
            ratio = jnp.where(sub > k, columns[k] * pivot_inverse, 0.0)
            inverse = jnp.where(sub == k, pivot_inverse, inverse)
            pivot_row = row(current, k)
            current = current - ratio * pivot_row
            tops = {i: row(columns[i], k) for i in range(k + 1, 8)}
            for i in range(k + 1, 8):
                columns[i] = columns[i] - ratio * tops[i]
            if not last:
                ratio = after_columns[k] * pivot_inverse
                for i in range(k + 1, 8):
                    after_columns[i] = after_columns[i] - ratio * tops[i]
                after = after - ratio * pivot_row
        out_ref[base : base + 8, :] = jnp.where(lane < base + 8, current * lax.sqrt(inverse), 0.0)
        if r < 14:
            top = base + 16
            scaled = jnp.where(lane >= top, current * inverse, 0.0)
            update = dot(scaled, current, 0, 0, precise)
            lanes = lax.broadcasted_iota(jnp.int32, (RANK - top, RANK), 1)
            rest = jnp.where((lanes >= base) & (lanes < base + 8), 0.0, work_ref[top:, :])
            work_ref[top:, :] = rest - update[top:, :]
        if not last:
            current = after


def orthonormal_kernel(core_ref, mine_ref, other_ref, out_ref, work_ref, inverse_ref):
    core = core_ref[0]
    mine, other = mine_ref[...], other_ref[...]
    gram = dot(mine, mine, 0, 0, precise) + dot(other, other, 0, 0, precise)
    invert_factor(gram, work_ref, inverse_ref)
    inverse = inverse_ref[...]
    for ref, part in ((mine_ref, core), (other_ref, 1 - core)):
        start = pl.multiple_of(part * HALF, HALF)
        out_ref[pl.ds(start, HALF), :] = split(dot(ref[...], inverse, 1, 1, precise))


def orthonormal(core, mine, other):
    return pl.pallas_call(
        orthonormal_kernel,
        out_shape=jax.ShapeDtypeStruct((DW, 2 * RANK), bf16),
        in_specs=[pl.BlockSpec(memory_space=pltpu.SMEM)]
        + [pl.BlockSpec(memory_space=pltpu.VMEM)] * 2,
        out_specs=pl.BlockSpec(memory_space=pltpu.VMEM),
        scratch_shapes=[pltpu.VMEM((RANK, RANK), f32), pltpu.VMEM((RANK, RANK), f32)],
        compiler_params=pltpu.CompilerParams(vmem_limit_bytes=32 * 2**20),
        cost_estimate=pl.CostEstimate(
            flops=2_000_000_000, bytes_accessed=4_000_000, transcendentals=256
        ),
        name="orthonormal",
    )(core, mine, other)


def factor_kernel(error_ref, slopes_ref, tokens_ref, p_ref, out_ref, y_ref):
    step = pl.program_id(0)

    @pl.when(step == 0)
    def _():
        y_ref[...] = split(folded(dot(tokens_ref[...], p_ref[...], 1, 0)))

    terms = dot(error_ref[...], p_ref[...], 1, 0) + dot(slopes_ref[...], y_ref[...], 1, 0)
    rows = lax.broadcasted_iota(jnp.int32, (TILE, RANK), 0) + step * TILE
    out_ref[...] = jnp.where(rows < HIDDEN, folded(terms), 0.0).astype(bf16)


def factor_terms(error, slopes, tokens, p_both):
    return pl.pallas_call(
        factor_kernel,
        grid=(4,),
        out_shape=jax.ShapeDtypeStruct((4 * TILE, RANK), bf16),
        in_specs=[
            pl.BlockSpec((TILE, DW), lambda i: (i, 0)),
            pl.BlockSpec((TILE, 256), lambda i: (i, 0)),
            whole((256, DW)),
            whole((DW, 2 * RANK)),
        ],
        out_specs=pl.BlockSpec((TILE, RANK), lambda i: (i, 0)),
        scratch_shapes=[pltpu.VMEM((256, 2 * RANK), bf16)],
        compiler_params=pltpu.CompilerParams(vmem_limit_bytes=32 * 2**20),
        cost_estimate=pl.CostEstimate(
            flops=2 * 1024 * DW * 256, bytes_accessed=8_000_000, transcendentals=0
        ),
        name="factor_terms",
    )(error, slopes, tokens, p_both)


def residual_kernel(error_ref, slopes_ref, tokens_ref, p_ref, q_ref, out_ref, factor_ref):
    q = q_ref[...]
    factor_ref[...] = q.astype(f32)
    values = error_ref[...].astype(f32) + dot(slopes_ref[...], tokens_ref[...], 1, 0)
    values = values - dot(jnp.concatenate([q, q], axis=1), p_ref[...], 1, 1)
    out_ref[...] = values.astype(bf16)


def residual(error, slopes, tokens, p_both, q_factor):
    return pl.pallas_call(
        residual_kernel,
        grid=(4,),
        out_shape=(
            jax.ShapeDtypeStruct((HIDDEN, DW), bf16),
            jax.ShapeDtypeStruct((HIDDEN, RANK), f32),
        ),
        in_specs=[
            pl.BlockSpec((TILE, DW), lambda i: (i, 0)),
            pl.BlockSpec((TILE, 256), lambda i: (i, 0)),
            whole((256, DW)),
            whole((DW, 2 * RANK)),
            pl.BlockSpec((TILE, RANK), lambda i: (i, 0)),
        ],
        out_specs=[
            pl.BlockSpec((TILE, DW), lambda i: (i, 0)),
            pl.BlockSpec((TILE, RANK), lambda i: (i, 0)),
        ],
        compiler_params=pltpu.CompilerParams(vmem_limit_bytes=48 * 2**20),
        cost_estimate=pl.CostEstimate(
            flops=4 * 1024 * DW * 256, bytes_accessed=14_000_000, transcendentals=0
        ),
        name="residual",
    )(error, slopes, tokens, p_both, q_factor)


def on_device(inputs, pre_act, grad_hidden, up_weight, error_in, q_prev):
    replicas = lax.axis_size("replica")
    core = (lax.axis_index("tensor") % 2).astype(jnp.int32)
    flag = core.reshape(1)
    error = error_in[0].T
    with jax.named_scope("gathers"):
        weights = lax.all_gather(up_weight, "replica", axis=0, tiled=True)
        mine = broadcast_exchange(inputs, 4, "tensor", X_GROUPS)
        other = lax.ppermute(mine, "tensor", CORE_PAIRS)
    with jax.named_scope("basis"):
        slopes = hidden_slope(pre_act.T, grad_hidden.T)
        q_both = split_outside(q_prev)
        slope_terms = folded(dot(slopes, q_both, 0, 0))
        error_terms = folded(dot(error, q_both, 0, 0))
        kept, sent, tokens = left_terms(flag, mine, other, slope_terms, error_terms)
        kept = kept + lax.ppermute(sent, "tensor", CORE_PAIRS)
        rows = lax.all_to_all(
            kept.reshape(16, HALF // 16, RANK), BOTH, 0, 0, axis_index_groups=XY_GROUPS
        )
        rows = jnp.sum(rows, axis=0)
        rows = jnp.sum(broadcast_exchange(rows, 8, "replica", Z_GROUPS), axis=0) / replicas
        mine = broadcast_exchange(rows, 16, BOTH, XY_GROUPS).reshape(HALF, RANK)
        other = lax.ppermute(mine, "tensor", CORE_PAIRS)
    p_both = orthonormal(flag, mine, other)
    with jax.named_scope("right_factor"):
        terms = factor_terms(error, slopes, tokens, p_both).reshape(32, 32, RANK)
        terms = lax.all_to_all(terms, "replica", 0, 0)
        block = jnp.sum(terms.astype(f32), axis=0) / replicas
        q_block = broadcast_exchange(block.astype(bf16), 32, "replica").reshape(1024, RANK)
    error_out, q_factor = residual(error, slopes, tokens, p_both, q_block)
    with jax.named_scope("input_grad"):
        partial_grad = dot(slopes, weights, 0, 1).reshape(4, 2, 32, DW)
        own = lax.dynamic_index_in_dim(partial_grad, core, 1, keepdims=False)
        pair = lax.dynamic_index_in_dim(partial_grad, 1 - core, 1, keepdims=False)
        own = (own + lax.ppermute(pair, "tensor", CORE_PAIRS)).reshape(128, DW)
        input_grad = lax.psum_scatter(
            own, "tensor", scatter_dimension=0, tiled=True, axis_index_groups=X_GROUPS
        ).astype(bf16)
    return (input_grad, q_factor, error_out.T[None])


def solution(mesh):
    placed = (
        P(("replica", "tensor"), None),
        P("replica", "tensor"),
        P("replica", "tensor"),
        P("replica", "tensor"),
        P("replica", None, "tensor"),
        P("tensor", None),
    )
    return jax.shard_map(
        on_device,
        mesh=mesh,
        in_specs=placed,
        out_specs=(P(("replica", "tensor"), None), P("tensor", None), P("replica", None, "tensor")),
        check_vma=False,
    )
```

time: 546 us -> 207 us (0.38); the launches traced: 536 us -> 206 us
  waiting for transfers between devices: 432 us -> 91.9 us
  matrix products: 58.3 us -> 10.5 us
  blocking collectives: 0 us -> 34.4 us
  starting transfers between devices: 0.37 us -> 20.1 us
  Pallas kernels: 0 us -> 18.3 us
  other arithmetic: 25.5 us -> 8.13 us
    psum x2 -> x0, waiting for transfers between devices: 400 us -> none  [the longest x1 262 us: on_device(): basis_sum = lax.psum(local_basis, ('replica', 'tensor')) / replicas]
    dot_general x6 -> x3, matrix products: 57 us -> 10.5 us  [dot(): lax.dot_general(left, right, (((left_dim,), (right_dim,)), ((), ())), pre...]
    all_to_all x0 -> x2, blocking collectives: none -> 34.4 us  [the longest x1 17.9 us: on_device(): terms = lax.all_to_all(terms, 'replica', 0, 0)]
    all_gather x2 -> x1, waiting for transfers between devices: 31.1 us -> 61.4 us  [on_device(): weights = lax.all_gather(up_weight, 'replica', axis=0, tiled=True)]
    all_to_all x0 -> x4, waiting for transfers between devices: none -> 25.6 us  [the longest x3 25.6 us: broadcast_exchange(): return lax.all_to_all(blocks, axis, 0, 0, axis_index_groups=groups)]
    another operation x5 -> x0, other arithmetic: 22.9 us -> none  [the longest x3 12.4 us: on_device(): factor = jnp.linalg.cholesky(gram_matrix)]
    all_to_all x0 -> x4, starting transfers between devices: none -> 19.7 us  [the longest x3 14.5 us: broadcast_exchange(): return lax.all_to_all(blocks, axis, 0, 0, axis_index_groups=groups)]
    pallas_call x0 -> x4, Pallas kernels: none -> 18.3 us  [the longest x1 7.18 us: orthonormal(): pl.pallas_call(orthonormal_kernel, out_shape=jax.ShapeDtypeStruct((DW, 2...]
  transfers between devices with their start and end apart: 5 -> 10, of which waited for: 3 -> 7; matrix products, arithmetic and copies ran while one was open for 11% -> 10% of each run, Pallas kernels for 0% -> 9%
where the time goes in v2:
time: 207 us; the launch traced here: 206 us
  waiting for transfers between devices  91.9 us (44%)
  blocking collectives  34.4 us (17%)
  starting transfers between devices  20.1 us (10%)
  Pallas kernels  18.3 us (9%)
  between operations  14.2 us (7%)
  matrix products  10.5 us (5%)
  local copies, waits for them, and re-layouts  8.62 us (4%)
  other arithmetic  8.13 us (4%)
    all_gather x1, waiting for transfers between devices, on_device(): weights = lax.all_gather(up_weight, 'replica', axis=0, tiled=True)  61.4 us
    all_to_all x3, waiting for transfers between devices, broadcast_exchange(): return lax.all_to_all(blocks, axis, 0, 0, axis_index_groups=groups)  25.6 us
    all_to_all x1, blocking collectives, on_device(): terms = lax.all_to_all(terms, 'replica', 0, 0)  17.9 us
    all_to_all x1, blocking collectives, broadcast_exchange(): return lax.all_to_all(blocks, axis, 0, 0, axis_index_groups=groups)  16.5 us
    all_to_all x3, starting transfers between devices, broadcast_exchange(): return lax.all_to_all(blocks, axis, 0, 0, axis_index_groups=groups)  14.5 us
    dot_general x3, matrix products, dot(): lax.dot_general(left, right, (((left_dim,), (right_dim,)), ((), ())), pre...  10.5 us
    pallas_call x1, Pallas kernels, orthonormal(): pl.pallas_call(orthonormal_kernel, out_shape=jax.ShapeDtypeStruct((DW, 2...  7.18 us
    pallas_call x1, Pallas kernels, residual(): pl.pallas_call(residual_kernel, grid=(4,), out_shape=(jax.ShapeDtypeStruc...  6.87 us
  transfers between devices with their start and end apart: 10, of which 7 were waited for; matrix products, arithmetic and copies ran while one was open for 10% of the time, Pallas kernels for 9%

profile of v2, /device:TPU:32, one launch (start us, length us, event | category | flops | bytes accessed | tf_op | source)
XLA Modules:
  0.0 206.1 jit_solution(5542935476795487808)
XLA Ops:
  7.2 0.7 all-gather.2.cloned.1.call-update
  7.9 1.8 broadcast_in_dim.10
  9.8 4.3 %all-to-all-start = ((bf16[4,32,2560]{2,1,0:T(8,128)(2,1)}), bf16[4,32,2560]{2,1,0:T(8,128)(2,1)S(1)}, u32[]{:S(2)}, u32[]{:S(2)}) async-start(bf16[4,32,2560]{2,1,0:T(8,128)(2,1)} %broadcast_in_dim.10), calls=%async_computation.1 | async-start | bytes 1310720 | tf_op jit(solution)/shard_map/gathers/all_to_all | solution.py:62
  14.2 0.5 fusion.10.slopes_ref
  14.7 0.3 fusion.15
  15.0 6.1 %fusion.2 = f32[2560,256]{1,0:T(8,128)} fusion(bf16[1,2560,992]{1,2,0:T(8,128)(2,1)} %param.10, bf16[992,128]{1,0:T(8,128)(2,1)S(1)} %get-tuple-element.14, bf16[992,128]{1,0:T(8,128)(2,1)S(1)} %get-tuple-element.13), kind=kOutput, calls=%fused_computation.2 | convolution fusion | flops 1301250048 | bytes 8208384 | tf_op jit(solution)/shard_map/basis/dot_general | solution.py:37
  21.1 3.8 %all-to-all-done.mine_ref = bf16[4,32,2560]{2,1,0:T(8,128)(2,1)S(1)} async-done(((bf16[4,32,2560]{2,1,0:T(8,128)(2,1)}), bf16[4,32,2560]{2,1,0:T(8,128)(2,1)S(1)}, u32[]{:S(2)}, u32[]{:S(2)}) %all-to-all-start) | async-done | bytes 655392 | tf_op jit(solution)/shard_map/gathers/all_to_all | solution.py:62
  24.9 1.9 slice_add_fusion.error_ref
  27.0 1.5 left_terms.1
  28.5 0.3 collective-permute-start.2
  28.9 2.0 collective-permute-done.2
  30.8 0.9 add.44
  31.8 5.2 %all-to-all-start.1 = ((f32[16,80,128]{2,1,0:T(8,128)}), f32[16,80,128]{2,1,0:T(8,128)S(1)}, u32[]{:S(2)}, u32[]{:S(2)}) async-start(f32[16,80,128]{2,1,0:T(8,128)} %bitcast.48), calls=%async_computation.2 | async-start | bytes 1310720 | tf_op jit(solution)/shard_map/basis/all_to_all | solution.py:261
  37.0 61.4 %all-gather.2.cloned.1.call-done = bf16[2560,992]{1,0:T(8,128)(2,1)} async-done(((bf16[80,992]{1,0:T(8,128)(2,1)}), bf16[2560,992]{1,0:T(8,128)(2,1)}) %all-gather.2.cloned.1.call-update) | async-done | bytes 5079056 | tf_op jit(solution)/shard_map/gathers/all_gather | solution.py:251
  98.3 4.1 %fusion.18 = f32[256,2560]{1,0:T(8,128)S(1)} fusion(bf16[992,256]{1,0:T(8,128)(2,1)S(1)} %fusion.10.slopes_ref, bf16[2560,992]{1,0:T(8,128)(2,1)} %all-gather.2.cloned.1.call-done), kind=kOutput, calls=%fused_computation.28 | convolution fusion | flops 1300234240 | bytes 8208384 | tf_op jit(solution)/shard_map/input_grad/dot_general | solution.py:37
  102.4 1.5 copy-done.1
  103.9 1.1 dynamic-slice_bitcast_fusion
  105.1 0.7 broadcast_in_dim.11
  105.8 4.6 %all-to-all-start.2 = ((f32[8,80,128]{2,1,0:T(8,128)}), f32[8,80,128]{2,1,0:T(8,128)S(1)}, u32[]{:S(2)}, u32[]{:S(2)}) async-start(f32[8,80,128]{2,1,0:T(8,128)} %broadcast_in_dim.11), calls=%async_computation.3 | async-start | bytes 655360 | tf_op jit(solution)/shard_map/basis/all_to_all | solution.py:62
  110.5 12.5 %all-to-all-done.2 = f32[8,80,128]{2,1,0:T(8,128)S(1)} async-done(((f32[8,80,128]{2,1,0:T(8,128)}), f32[8,80,128]{2,1,0:T(8,128)S(1)}, u32[]{:S(2)}, u32[]{:S(2)}) %all-to-all-start.2) | async-done | bytes 327712 | tf_op jit(solution)/shard_map/basis/all_to_all | solution.py:62
  123.0 0.9 broadcast_in_dim.12
  123.9 5.6 %all-to-all-start.3 = ((f32[16,80,128]{2,1,0:T(8,128)}), f32[16,80,128]{2,1,0:T(8,128)S(1)}, u32[]{:S(2)}, u32[]{:S(2)}) async-start(f32[16,80,128]{2,1,0:T(8,128)} %broadcast_in_dim.12), calls=%async_computation.4 | async-start | bytes 1310720 | tf_op jit(solution)/shard_map/basis/all_to_all | solution.py:62
  129.5 2.9 %bitcast_add_fusion = f32[4,32,2560]{2,1,0:T(8,128)} fusion(f32[4,32,2560]{2,1,0:T(8,128)} %collective-permute-done, f32[4,2,32,2560]{3,2,1,0:T(8,128)} %bitcast.47, s32[]{:T(128)S(6)} %select_n.15), kind=kLoop, calls=%fused_computation.5 | loop fusion | flops 327680 | bytes 3932164 | tf_op jit(solution)/shard_map/input_grad/add | solution.py:279
  132.5 9.3 %all-to-all-done.3 = f32[16,80,128]{2,1,0:T(8,128)S(1)} async-done(((f32[16,80,128]{2,1,0:T(8,128)}), f32[16,80,128]{2,1,0:T(8,128)S(1)}, u32[]{:S(2)}, u32[]{:S(2)}) %all-to-all-start.3) | async-done | bytes 655392 | tf_op jit(solution)/shard_map/basis/all_to_all | solution.py:62
  141.8 2.1 %collective-permute-done.3.other_ref = f32[1280,128]{1,0:T(8,128)S(1)} collective-permute-done((f32[1280,128]{1,0:T(8,128)S(1)}, f32[1280,128]{1,0:T(8,128)S(1)}, u32[]{:S(2)}, u32[]{:S(2)}) %collective-permute-start.3) | collective-permute-done | bytes 655392 | tf_op jit(solution)/shard_map/basis/ppermute | solution.py:267
  143.9 7.2 %orthonormal.1.p_ref = bf16[2560,256]{1,0:T(8,128)(2,1)S(1)} custom-call(s32[1]{0:T(128)} %bitcast.8.core_ref, f32[1280,128]{1,0:T(8,128)S(1)} %bitcast.43, f32[1280,128]{1,0:T(8,128)S(1)} %collective-permute-done.3.other_ref), custom_call_target="tpu_custom_call" | custom-call | flops 2000000000 | bytes 4000000 | tf_op jit(solution)/shard_map/orthonormal/pallas_call | solution.py:162
  151.1 2.5 %copy-done = bf16[1,2560,992]{1,2,0:T(8,128)(2,1)S(1)} copy-done((bf16[1,2560,992]{1,2,0:T(8,128)(2,1)S(1)}, bf16[1,2560,992]{1,2,0:T(8,128)(2,1)}, u32[]{:S(2)}) %copy-start) | copy-done | bytes 5079064
  153.5 2.7 %factor_terms.1 = bf16[1024,128]{1,0:T(8,128)(2,1)S(1)} custom-call(bf16[992,2560]{1,0:T(8,128)(2,1)S(1)} %bitcast.40, bf16[992,256]{1,0:T(8,128)(2,1)S(1)} %fusion.10.slopes_ref, bf16[256,2560]{1,0:T(8,128)(2,1)S(1)} %get-tuple-element.8.tokens_ref, bf16[2560,256]{1,0:T(8,128)(2,1)S(1)} %orthonormal.1.p_ref), custom_call_target="tpu_custom_call" | custom-call | flops 1342177280 | bytes 8000000 | tf_op jit(solution)/shard_map/right_factor/factor_terms/pallas_call | solution.py:190
  156.3 17.9 %all_to_all.30 = bf16[32,32,128]{2,1,0:T(8,128)(2,1)S(1)} all-to-all(bf16[32,32,128]{2,1,0:T(8,128)(2,1)S(1)} %bitcast.41), channel_id=1, replica_groups=mesh['replica'=32,'tensor'=8] {'replica'}, dimensions={0} | all-to-all | bytes 524288 | tf_op jit(solution)/shard_map/right_factor/all_to_all | solution.py:271
  174.3 16.5 %all_to_all.31 = bf16[32,32,128]{2,1,0:T(8,128)(2,1)S(1)} all-to-all(bf16[32,32,128]{2,1,0:T(8,128)(2,1)S(1)} %broadcast_in_dim.13), channel_id=1, replica_groups=mesh['replica'=32,'tensor'=8] {'replica'}, dimensions={0} | all-to-all | bytes 524288 | tf_op jit(solution)/shard_map/right_factor/all_to_all | solution.py:62
  190.8 6.9 %residual.1 = (bf16[992,2560]{1,0:T(8,128)(2,1)}, f32[992,128]{1,0:T(8,128)}) custom-call(bf16[992,2560]{1,0:T(8,128)(2,1)} %bitcast.39, bf16[992,256]{1,0:T(8,128)(2,1)S(1)} %fusion.10.slopes_ref, bf16[256,2560]{1,0:T(8,128)(2,1)S(1)} %get-tuple-element.8.tokens_ref, bf16[2560,256]{1,0:T(8,128)(2,1)S(1)} %orthonormal.1.p_ref, bf16[1024,128]{1,0:T(8,128)(2,1)S(1)} %bitcast.44), custom_call_target="tpu_custom_call" | custom-call | flops 2684354560 | bytes 14000000 | tf_op jit(solution)/shard_map/residual/pallas_call | solution.py:219
  197.7 1.7 convert_element_type.39
  (26 shorter events, 0.6 us)
Async XLA Ops:
  7.2 6.9 %copy-start.4 = (f32[992,128]{1,0:T(8,128)S(1)}, f32[992,128]{1,0:T(8,128)}, u32[]{:S(2)}) copy-start(f32[992,128]{1,0:T(8,128)} %param.11) | copy-start | bytes 1523716
  7.2 7.0 %copy-start.3 = (bf16[256,992]{0,1:T(8,128)(2,1)S(1)}, bf16[256,992]{0,1:T(8,128)(2,1)}, u32[]{:S(2)}) copy-start(bf16[256,992]{0,1:T(8,128)(2,1)} %param.8) | copy-start | bytes 1523716
  7.2 7.0 %copy-start.2 = (bf16[256,992]{0,1:T(8,128)(2,1)S(1)}, bf16[256,992]{0,1:T(8,128)(2,1)}, u32[]{:S(2)}) copy-start(bf16[256,992]{0,1:T(8,128)(2,1)} %param.7) | copy-start | bytes 1523716
  7.2 91.1 %all-gather.2.cloned.1.call-start = ((), (), s32[]{:S(2)}) async-start(), calls=%async_computation.7 | async-start | bytes 5406720 | tf_op jit(solution)/shard_map/gathers/all_gather | solution.py:251
  9.8 15.2 %all-to-all-start = ((bf16[4,32,2560]{2,1,0:T(8,128)(2,1)}), bf16[4,32,2560]{2,1,0:T(8,128)(2,1)S(1)}, u32[]{:S(2)}, u32[]{:S(2)}) async-start(bf16[4,32,2560]{2,1,0:T(8,128)(2,1)} %broadcast_in_dim.10), calls=%async_computation.1 | async-start | bytes 1310720 | tf_op jit(solution)/shard_map/gathers/all_to_all | solution.py:62
  24.9 2.1 %collective-permute-start.1 = (bf16[4,32,2560]{2,1,0:T(8,128)(2,1)S(1)}, bf16[4,32,2560]{2,1,0:T(8,128)(2,1)S(1)}, u32[]{:S(2)}, u32[]{:S(2)}) collective-permute-start(bf16[4,32,2560]{2,1,0:T(8,128)(2,1)S(1)} %all-to-all-done.mine_ref), channel_id=1, source_target_pairs={{0,1},{1,0},{2,3},{3,2},{4,5},{5,4},{6,7},{7,6},{8,9},{9,8},{10,11... | collective-permute-start | bytes 1966088 | tf_op jit(solution)/shard_map/gathers/ppermute | solution.py:253
  28.5 2.3 %collective-permute-start.2 = (f32[1280,128]{1,0:T(8,128)}, f32[1280,128]{1,0:T(8,128)S(1)}, u32[]{:S(2)}, u32[]{:S(2)}) collective-permute-start(f32[1280,128]{1,0:T(8,128)} %get-tuple-element.10), channel_id=1, source_target_pairs={{0,1},{1,0},{2,3},{3,2},{4,5},{5,4},{6,7},{7,6},{8,9},{9,8},{10,11... | collective-permute-start | bytes 1966088 | tf_op jit(solution)/shard_map/basis/ppermute | solution.py:260
  31.8 73.3 %all-to-all-start.1 = ((f32[16,80,128]{2,1,0:T(8,128)}), f32[16,80,128]{2,1,0:T(8,128)S(1)}, u32[]{:S(2)}, u32[]{:S(2)}) async-start(f32[16,80,128]{2,1,0:T(8,128)} %bitcast.48), calls=%async_computation.2 | async-start | bytes 1310720 | tf_op jit(solution)/shard_map/basis/all_to_all | solution.py:261
  102.4 1.5 copy-start.1
  105.0 24.5 %collective-permute-start = (f32[4,32,2560]{2,1,0:T(8,128)}, f32[4,32,2560]{2,1,0:T(8,128)}, u32[]{:S(2)}, u32[]{:S(2)}) collective-permute-start(f32[4,32,2560]{2,1,0:T(8,128)} %dynamic-slice_bitcast_fusion), channel_id=1, source_target_pairs={{0,1},{1,0},{2,3},{3,2},{4,5},{5,4},{6,7},{7,6},{8,9},{9,8},{10,11... | collective-permute-start | bytes 3932168 | tf_op jit(solution)/shard_map/input_grad/ppermute | solution.py:279
  105.8 17.1 %all-to-all-start.2 = ((f32[8,80,128]{2,1,0:T(8,128)}), f32[8,80,128]{2,1,0:T(8,128)S(1)}, u32[]{:S(2)}, u32[]{:S(2)}) async-start(f32[8,80,128]{2,1,0:T(8,128)} %broadcast_in_dim.11), calls=%async_computation.3 | async-start | bytes 655360 | tf_op jit(solution)/shard_map/basis/all_to_all | solution.py:62
  123.9 17.9 %all-to-all-start.3 = ((f32[16,80,128]{2,1,0:T(8,128)}), f32[16,80,128]{2,1,0:T(8,128)S(1)}, u32[]{:S(2)}, u32[]{:S(2)}) async-start(f32[16,80,128]{2,1,0:T(8,128)} %broadcast_in_dim.12), calls=%async_computation.4 | async-start | bytes 1310720 | tf_op jit(solution)/shard_map/basis/all_to_all | solution.py:62
  129.5 68.2 %reduce-scatter.2.cloned.1.call-start = ((), (), s32[]{:S(2)}) async-start(), calls=%async_computation.8 | async-start | bytes 1638400 | tf_op jit(solution)/shard_map/input_grad/reduce_scatter | solution.py:280
  141.8 2.1 %collective-permute-start.3 = (f32[1280,128]{1,0:T(8,128)S(1)}, f32[1280,128]{1,0:T(8,128)S(1)}, u32[]{:S(2)}, u32[]{:S(2)}) collective-permute-start(f32[1280,128]{1,0:T(8,128)S(1)} %bitcast.42), channel_id=1, source_target_pairs={{0,1},{1,0},{2,3},{3,2},{4,5},{5,4},{6,7},{7,6},{8,9},{9,8},{10,11... | collective-permute-start | bytes 1966088 | tf_op jit(solution)/shard_map/basis/ppermute | solution.py:267
  151.1 2.5 %copy-start = (bf16[1,2560,992]{1,2,0:T(8,128)(2,1)S(1)}, bf16[1,2560,992]{1,2,0:T(8,128)(2,1)}, u32[]{:S(2)}) copy-start(bf16[1,2560,992]{1,2,0:T(8,128)(2,1)} %param.10) | copy-start | bytes 15237124
Sparse Core Ops, SparseCore 0:
  10.6 87.6 all-gather.1
  132.9 24.5 reduce-scatter.1

commit v3 on v2

--- a/solution.py
+++ b/solution.py
@@ -15,6 +15,7 @@
 HALF = DW // 2
 HIDDEN = 992
 TILE = 256
+LARGE = 60 * 2**20
 CORE_PAIRS = [(i, i ^ 1) for i in range(8)]
 X_GROUPS = [[core + 2 * x for x in range(4)] for core in range(2)]
 XY_GROUPS = [
@@ -66,36 +67,83 @@
     return pl.BlockSpec(shape, lambda *_: (0,) * len(shape), memory_space=memory)
 
 
-def terms_kernel(core_ref, mine_ref, other_ref, z_ref, error_ref, kept_ref, sent_ref, tokens_ref):
+def after(values, order):
+    return pl.pallas_call(
+        lambda values_ref, order_ref, out_ref: None,
+        out_shape=jax.ShapeDtypeStruct(values.shape, values.dtype),
+        in_specs=[pl.BlockSpec(memory_space=pl.ANY)] * 2,
+        out_specs=pl.BlockSpec(memory_space=pl.ANY),
+        input_output_aliases={0: 0},
+        cost_estimate=pl.CostEstimate(flops=1000, bytes_accessed=1000, transcendentals=0),
+        name="after",
+    )(values, order)
+
+
+def front_kernel(core_ref, error_ref, slopes_ref, q_ref, error_out_ref, own_ref, pair_ref, z_ref):
     core = core_ref[0]
-    for x in range(4):
-        for ref, owner in ((mine_ref, core), (other_ref, 1 - core)):
-            start = pl.multiple_of((2 * x + owner) * 32, 32)
-            tokens_ref[pl.ds(start, 32), :] = ref[x]
-    both = split(z_ref[...])
+
+    @pl.when(pl.program_id(0) == 0)
+    def _():
+        z_ref[...] = folded(dot(slopes_ref[...], q_ref[...], 0, 0))
+        for x in range(4):
+            for ref, owner in ((own_ref, core), (pair_ref, 1 - core)):
+                start = pl.multiple_of((2 * x + owner) * 32, 32)
+                ref[32 * x : 32 * x + 32, :] = z_ref[pl.ds(start, 32), :]
+
+    error_out_ref[...] = folded(dot(error_ref[...], q_ref[...], 0, 0))
+
+
+def front_terms(core, error, slopes, q_both):
+    here = pl.BlockSpec(memory_space=pltpu.VMEM)
+    return pl.pallas_call(
+        front_kernel,
+        grid=(5,),
+        out_shape=(
+            jax.ShapeDtypeStruct((DW, RANK), f32),
+            jax.ShapeDtypeStruct((128, RANK), f32),
+            jax.ShapeDtypeStruct((128, RANK), f32),
+        ),
+        in_specs=[
+            pl.BlockSpec(memory_space=pltpu.SMEM),
+            pl.BlockSpec((HIDDEN, 512), lambda i: (0, i)),
+            here,
+            here,
+        ],
+        out_specs=[pl.BlockSpec((512, RANK), lambda i: (i, 0)), here, here],
+        scratch_shapes=[pltpu.VMEM((256, RANK), f32)],
+        compiler_params=pltpu.CompilerParams(vmem_limit_bytes=LARGE),
+        cost_estimate=pl.CostEstimate(
+            flops=2 * HIDDEN * DW * 256, bytes_accessed=7_000_000, transcendentals=0
+        ),
+        name="front_terms",
+    )(core, error, slopes, q_both)
+
+
+def terms_kernel(core_ref, mine_ref, own_ref, got_ref, error_ref, kept_ref, sent_ref):
+    core = core_ref[0]
+    both = split(own_ref[...] + got_ref[...])
     for ref, part in ((kept_ref, core), (sent_ref, 1 - core)):
         start = pl.multiple_of(part * HALF, HALF)
-        columns = tokens_ref[:, pl.ds(start, HALF)]
+        columns = mine_ref[:, pl.ds(start, HALF)]
         ref[...] = folded(dot(columns, both, 0, 0)) + error_ref[pl.ds(start, HALF), :]
 
 
-def left_terms(core, mine, other, slope_terms, error_terms):
+def left_terms(core, mine, own, got, errors):
     return pl.pallas_call(
         terms_kernel,
         out_shape=(
             jax.ShapeDtypeStruct((HALF, RANK), f32),
             jax.ShapeDtypeStruct((HALF, RANK), f32),
-            jax.ShapeDtypeStruct((256, DW), bf16),
         ),
         in_specs=[pl.BlockSpec(memory_space=pltpu.SMEM)]
         + [pl.BlockSpec(memory_space=pltpu.VMEM)] * 4,
-        out_specs=[pl.BlockSpec(memory_space=pltpu.VMEM)] * 3,
-        compiler_params=pltpu.CompilerParams(vmem_limit_bytes=32 * 2**20),
-        cost_estimate=pl.CostEstimate(
-            flops=2 * 256 * DW * 256, bytes_accessed=6_000_000, transcendentals=0
+        out_specs=[pl.BlockSpec(memory_space=pltpu.VMEM)] * 2,
+        compiler_params=pltpu.CompilerParams(vmem_limit_bytes=20 * 2**20),
+        cost_estimate=pl.CostEstimate(
+            flops=2 * 128 * DW * 256, bytes_accessed=4_000_000, transcendentals=0
         ),
         name="left_terms",
-    )(core, mine, other, slope_terms, error_terms)
+    )(core, mine, own, got, errors)
 
 
 def invert_factor(gram, work_ref, out_ref):
@@ -166,7 +214,7 @@
         + [pl.BlockSpec(memory_space=pltpu.VMEM)] * 2,
         out_specs=pl.BlockSpec(memory_space=pltpu.VMEM),
         scratch_shapes=[pltpu.VMEM((RANK, RANK), f32), pltpu.VMEM((RANK, RANK), f32)],
-        compiler_params=pltpu.CompilerParams(vmem_limit_bytes=32 * 2**20),
+        compiler_params=pltpu.CompilerParams(vmem_limit_bytes=20 * 2**20),
         cost_estimate=pl.CostEstimate(
             flops=2_000_000_000, bytes_accessed=4_000_000, transcendentals=256
         ),
@@ -174,72 +222,161 @@
     )(core, mine, other)
 
 
-def factor_kernel(error_ref, slopes_ref, tokens_ref, p_ref, out_ref, y_ref):
+def factor_kernel(
+    core_ref, error_ref, slopes_ref, mine_ref, other_ref, p_ref, *refs
+):
+    out_ref, turned_ref, tokens_ref, y_ref = refs[-4:]
     step = pl.program_id(0)
+    core = core_ref[0]
 
     @pl.when(step == 0)
     def _():
+        for x in range(4):
+            for ref, owner in ((mine_ref, core), (other_ref, 1 - core)):
+                start = pl.multiple_of((2 * x + owner) * 32, 32)
+                tokens_ref[pl.ds(start, 32), :] = ref[32 * x : 32 * x + 32, :]
         y_ref[...] = split(folded(dot(tokens_ref[...], p_ref[...], 1, 0)))
 
+    turned_ref[...] = p_ref[pl.ds(pl.multiple_of(step * 640, 640), 640), :].T
     terms = dot(error_ref[...], p_ref[...], 1, 0) + dot(slopes_ref[...], y_ref[...], 1, 0)
     rows = lax.broadcasted_iota(jnp.int32, (TILE, RANK), 0) + step * TILE
     out_ref[...] = jnp.where(rows < HIDDEN, folded(terms), 0.0).astype(bf16)
 
 
-def factor_terms(error, slopes, tokens, p_both):
+def factor_terms(core, error, slopes, mine, other, p_both, *order):
+    here = pl.BlockSpec(memory_space=pltpu.VMEM)
     return pl.pallas_call(
         factor_kernel,
         grid=(4,),
-        out_shape=jax.ShapeDtypeStruct((4 * TILE, RANK), bf16),
+        out_shape=(
+            jax.ShapeDtypeStruct((4 * TILE, RANK), bf16),
+            jax.ShapeDtypeStruct((2 * RANK, DW), bf16),
+            jax.ShapeDtypeStruct((256, DW), bf16),
+        ),
         in_specs=[
+            pl.BlockSpec(memory_space=pltpu.SMEM),
             pl.BlockSpec((TILE, DW), lambda i: (i, 0)),
             pl.BlockSpec((TILE, 256), lambda i: (i, 0)),
-            whole((256, DW)),
-            whole((DW, 2 * RANK)),
-        ],
-        out_specs=pl.BlockSpec((TILE, RANK), lambda i: (i, 0)),
+            here,
+            here,
+            here,
+        ]
+        + [pl.BlockSpec(memory_space=pl.ANY)] * len(order),
+        out_specs=(
+            pl.BlockSpec((TILE, RANK), lambda i: (i, 0)),
+            pl.BlockSpec((2 * RANK, 640), lambda i: (0, i)),
+            here,
+        ),
         scratch_shapes=[pltpu.VMEM((256, 2 * RANK), bf16)],
-        compiler_params=pltpu.CompilerParams(vmem_limit_bytes=32 * 2**20),
+        compiler_params=pltpu.CompilerParams(vmem_limit_bytes=20 * 2**20),
         cost_estimate=pl.CostEstimate(
             flops=2 * 1024 * DW * 256, bytes_accessed=8_000_000, transcendentals=0
         ),
         name="factor_terms",
-    )(error, slopes, tokens, p_both)
-
-
-def residual_kernel(error_ref, slopes_ref, tokens_ref, p_ref, q_ref, out_ref, factor_ref):
+    )(core, error, slopes, mine, other, p_both, *order)
+
+
+def residual_kernel(error_ref, slopes_ref, tokens_ref, turned_ref, q_ref, out_ref, factor_ref):
     q = q_ref[...]
     factor_ref[...] = q.astype(f32)
-    values = error_ref[...].astype(f32) + dot(slopes_ref[...], tokens_ref[...], 1, 0)
-    values = values - dot(jnp.concatenate([q, q], axis=1), p_ref[...], 1, 1)
-    out_ref[...] = values.astype(bf16)
-
-
-def residual(error, slopes, tokens, p_both, q_factor):
+    left = jnp.concatenate([slopes_ref[...], -q, -q], axis=1)
+    for i in range(DW // 512):
+        columns = slice(512 * i, 512 * i + 512)
+        right = jnp.concatenate([tokens_ref[:, columns], turned_ref[:, columns]], axis=0)
+        values = error_ref[:, columns].astype(f32) + dot(left, right, 1, 0)
+        out_ref[:, columns] = values.astype(bf16)
+
+
+def residual(error, slopes, tokens, turned, q_factor):
+    here = pl.BlockSpec(memory_space=pltpu.VMEM)
+    rows = 496
     return pl.pallas_call(
         residual_kernel,
-        grid=(4,),
+        grid=(HIDDEN // rows,),
         out_shape=(
             jax.ShapeDtypeStruct((HIDDEN, DW), bf16),
             jax.ShapeDtypeStruct((HIDDEN, RANK), f32),
         ),
         in_specs=[
-            pl.BlockSpec((TILE, DW), lambda i: (i, 0)),
-            pl.BlockSpec((TILE, 256), lambda i: (i, 0)),
-            whole((256, DW)),
-            whole((DW, 2 * RANK)),
-            pl.BlockSpec((TILE, RANK), lambda i: (i, 0)),
+            pl.BlockSpec((rows, DW), lambda i: (i, 0)),
+            pl.BlockSpec((rows, 256), lambda i: (i, 0)),
+            here,
+            here,
+            pl.BlockSpec((rows, RANK), lambda i: (i, 0)),
         ],
         out_specs=[
-            pl.BlockSpec((TILE, DW), lambda i: (i, 0)),
-            pl.BlockSpec((TILE, RANK), lambda i: (i, 0)),
+            pl.BlockSpec((rows, DW), lambda i: (i, 0)),
+            pl.BlockSpec((rows, RANK), lambda i: (i, 0)),
         ],
-        compiler_params=pltpu.CompilerParams(vmem_limit_bytes=48 * 2**20),
-        cost_estimate=pl.CostEstimate(
-            flops=4 * 1024 * DW * 256, bytes_accessed=14_000_000, transcendentals=0
+        compiler_params=pltpu.CompilerParams(vmem_limit_bytes=LARGE),
+        cost_estimate=pl.CostEstimate(
+            flops=4 * 1024 * DW * 256, bytes_accessed=12_000_000, transcendentals=0
         ),
         name="residual",
-    )(error, slopes, tokens, p_both, q_factor)
+    )(error, slopes, tokens, turned, q_factor)
+
+
+def mean_kernel(blocks_ref, out_ref):
+    mean = jnp.sum(blocks_ref[...].astype(f32), axis=0) / 32
+    out_ref[...] = jnp.broadcast_to(mean.astype(bf16)[None], out_ref.shape)
+
+
+def mean_copies(blocks):
+    here = pl.BlockSpec(memory_space=pltpu.VMEM)
+    return pl.pallas_call(
+        mean_kernel,
+        out_shape=jax.ShapeDtypeStruct(blocks.shape, bf16),
+        in_specs=[here],
+        out_specs=here,
+        compiler_params=pltpu.CompilerParams(vmem_limit_bytes=8 * 2**20),
+        cost_estimate=pl.CostEstimate(flops=200_000, bytes_accessed=600_000, transcendentals=0),
+        name="mean_copies",
+    )(blocks)
+
+
+def grad_kernel(core_ref, slopes_ref, weights_ref, order_ref, own_ref, pair_ref, full_ref):
+    del order_ref
+    core = core_ref[0]
+    full_ref[...] = dot(slopes_ref[...], weights_ref[...], 0, 1)
+    for x in range(4):
+        for ref, owner in ((own_ref, core), (pair_ref, 1 - core)):
+            start = pl.multiple_of((2 * x + owner) * 32, 32)
+            ref[32 * x : 32 * x + 32, :] = full_ref[pl.ds(start, 32), :]
+
+
+def grad_terms(core, slopes, weights, order):
+    width = 512
+    return pl.pallas_call(
+        grad_kernel,
+        grid=(DW // width,),
+        out_shape=(jax.ShapeDtypeStruct((128, DW), f32), jax.ShapeDtypeStruct((128, DW), f32)),
+        in_specs=[
+            pl.BlockSpec(memory_space=pltpu.SMEM),
+            pl.BlockSpec(memory_space=pltpu.VMEM),
+            pl.BlockSpec((width, HIDDEN), lambda i: (i, 0)),
+            pl.BlockSpec(memory_space=pl.ANY),
+        ],
+        out_specs=[pl.BlockSpec((128, width), lambda i: (0, i))] * 2,
+        scratch_shapes=[pltpu.VMEM((256, width), f32)],
+        compiler_params=pltpu.CompilerParams(vmem_limit_bytes=16 * 2**20),
+        cost_estimate=pl.CostEstimate(
+            flops=2 * 256 * HIDDEN * DW, bytes_accessed=8_000_000, transcendentals=0
+        ),
+        name="grad_terms",
+    )(core, slopes, weights, order)
+
+
+def token_owners_sum(own):
+    x = lax.axis_index("tensor") // 2
+
+    def block(step):
+        return lax.dynamic_index_in_dim(own, (x + step) % 4, 0, keepdims=False)
+
+    total = block(0)
+    for step in range(1, 4):
+        pairs = [(i, (i + 2 * step) % 8) for i in range(8)]
+        total = total + lax.ppermute(block(step).astype(bf16), "tensor", pairs).astype(f32)
+    return total.astype(bf16)
 
 
 def on_device(inputs, pre_act, grad_hidden, up_weight, error_in, q_prev):
@@ -249,37 +386,32 @@
     error = error_in[0].T
     with jax.named_scope("gathers"):
         weights = lax.all_gather(up_weight, "replica", axis=0, tiled=True)
-        mine = broadcast_exchange(inputs, 4, "tensor", X_GROUPS)
+        slopes = hidden_slope(pre_act.T, grad_hidden.T)
+        mine = broadcast_exchange(inputs, 4, "tensor", X_GROUPS).reshape(128, DW)
         other = lax.ppermute(mine, "tensor", CORE_PAIRS)
     with jax.named_scope("basis"):
-        slopes = hidden_slope(pre_act.T, grad_hidden.T)
         q_both = split_outside(q_prev)
-        slope_terms = folded(dot(slopes, q_both, 0, 0))
-        error_terms = folded(dot(error, q_both, 0, 0))
-        kept, sent, tokens = left_terms(flag, mine, other, slope_terms, error_terms)
+        errors, own, pair = front_terms(flag, error, slopes, q_both)
+        got = lax.ppermute(pair, "tensor", CORE_PAIRS)
+        kept, sent = left_terms(flag, mine, own, got, errors)
         kept = kept + lax.ppermute(sent, "tensor", CORE_PAIRS)
         rows = lax.all_to_all(
             kept.reshape(16, HALF // 16, RANK), BOTH, 0, 0, axis_index_groups=XY_GROUPS
         )
         rows = jnp.sum(rows, axis=0)
         rows = jnp.sum(broadcast_exchange(rows, 8, "replica", Z_GROUPS), axis=0) / replicas
-        mine = broadcast_exchange(rows, 16, BOTH, XY_GROUPS).reshape(HALF, RANK)
-        other = lax.ppermute(mine, "tensor", CORE_PAIRS)
-    p_both = orthonormal(flag, mine, other)
+        half = broadcast_exchange(rows, 16, BOTH, XY_GROUPS).reshape(HALF, RANK)
+    p_both = orthonormal(flag, half, lax.ppermute(half, "tensor", CORE_PAIRS))
     with jax.named_scope("right_factor"):
-        terms = factor_terms(error, slopes, tokens, p_both).reshape(32, 32, RANK)
-        terms = lax.all_to_all(terms, "replica", 0, 0)
-        block = jnp.sum(terms.astype(f32), axis=0) / replicas
-        q_block = broadcast_exchange(block.astype(bf16), 32, "replica").reshape(1024, RANK)
-    error_out, q_factor = residual(error, slopes, tokens, p_both, q_block)
+        terms, turned, tokens = factor_terms(flag, error, slopes, mine, other, p_both)
+        blocks = lax.all_to_all(terms.reshape(32, 32, RANK), "replica", 0, 0)
+        copies = mean_copies(blocks)
+        q_block = lax.all_to_all(copies, "replica", 0, 0).reshape(1024, RANK)
+    error_out, q_factor = residual(error, slopes, tokens, turned, q_block)
     with jax.named_scope("input_grad"):
-        partial_grad = dot(slopes, weights, 0, 1).reshape(4, 2, 32, DW)
-        own = lax.dynamic_index_in_dim(partial_grad, core, 1, keepdims=False)
-        pair = lax.dynamic_index_in_dim(partial_grad, 1 - core, 1, keepdims=False)
-        own = (own + lax.ppermute(pair, "tensor", CORE_PAIRS)).reshape(128, DW)
-        input_grad = lax.psum_scatter(
-            own, "tensor", scatter_dimension=0, tiled=True, axis_index_groups=X_GROUPS
-        ).astype(bf16)
+        own, pair = grad_terms(flag, slopes, weights, terms)
+        own = own + lax.ppermute(after(pair, copies), "tensor", CORE_PAIRS)
+        input_grad = token_owners_sum(own.reshape(4, 32, DW))
     return (input_grad, q_factor, error_out.T[None])
 
 

time: 207 us -> 159 us (0.77)
  waiting for transfers between devices: 91.9 us -> 12.4 us
  blocking collectives: 34.4 us -> 73.7 us
  matrix products: 10.5 us -> 0 us
  Pallas kernels: 18.3 us -> 28 us
  starting transfers between devices: 20.1 us -> 14.2 us
  other arithmetic: 8.13 us -> 4.58 us
  local copies, waits for them, and re-layouts: 8.62 us -> 10.9 us
    all_gather x1, waiting for transfers between devices: 61.4 us -> 0.01 us  [on_device(): weights = lax.all_gather(up_weight, 'replica', axis=0, tiled=True)]
    all_to_all x3 -> x1, waiting for transfers between devices: 25.6 us -> 0.01 us  [broadcast_exchange(): return lax.all_to_all(blocks, axis, 0, 0, axis_index_groups=groups)]
    all_to_all x1 -> x2, blocking collectives: 17.9 us -> 39.4 us  [the longest x1 20.7 us: on_device(): lax.all_to_all(kept.reshape(16, HALF // 16, RANK), BOTH, 0, 0, axis_index...]
    all_to_all x1 -> x2, blocking collectives: 16.5 us -> 34.3 us  [broadcast_exchange(): return lax.all_to_all(blocks, axis, 0, 0, axis_index_groups=groups)]
    pallas_call x2 -> x6, Pallas kernels: 9.61 us -> 20.2 us  [the longest x1 7.07 us: residual(): pl.pallas_call(residual_kernel, grid=(HIDDEN // rows,), out_shape=(jax.Sh...]
    dot_general x3 -> x0, matrix products: 10.5 us -> none  [dot(): lax.dot_general(left, right, (((left_dim,), (right_dim,)), ((), ())), pre...]
    all_to_all x3 -> x1, starting transfers between devices: 14.5 us -> 4.29 us  [broadcast_exchange(): return lax.all_to_all(blocks, axis, 0, 0, axis_index_groups=groups)]
    all_to_all x1, waiting for transfers between devices: 0.01 us -> 6.73 us  [on_device(): q_block = lax.all_to_all(copies, 'replica', 0, 0).reshape(1024, RANK)]
  transfers between devices with their start and end apart: 10 -> 11, of which waited for: 7 -> 4; matrix products, arithmetic and copies ran while one was open for 10% -> 4% of each run, Pallas kernels for 9% -> 16%
where the time goes in v3:
time: 159 us; the launch traced here: 158 us
  blocking collectives  73.7 us (46%)
  Pallas kernels  28 us (18%)
  between operations  14.3 us (9%)
  starting transfers between devices  14.2 us (9%)
  waiting for transfers between devices  12.4 us (8%)
  local copies, waits for them, and re-layouts  10.9 us (7%)
  other arithmetic  4.58 us (3%)
    all_to_all x2, blocking collectives, broadcast_exchange(): return lax.all_to_all(blocks, axis, 0, 0, axis_index_groups=groups)  34.3 us
    all_to_all x1, blocking collectives, on_device(): lax.all_to_all(kept.reshape(16, HALF // 16, RANK), BOTH, 0, 0, axis_index...  20.7 us
    all_to_all x1, blocking collectives, on_device(): blocks = lax.all_to_all(terms.reshape(32, 32, RANK), 'replica', 0, 0)  18.7 us
    unnamed x26, local copies, waits for them, and re-layouts  9.01 us
    pallas_call x1, Pallas kernels, orthonormal(): pl.pallas_call(orthonormal_kernel, out_shape=jax.ShapeDtypeStruct((DW, 2...  7.21 us
    pallas_call x1, Pallas kernels, residual(): pl.pallas_call(residual_kernel, grid=(HIDDEN // rows,), out_shape=(jax.Sh...  7.07 us
    all_to_all x1, waiting for transfers between devices, on_device(): q_block = lax.all_to_all(copies, 'replica', 0, 0).reshape(1024, RANK)  6.73 us
    pallas_call x1, Pallas kernels, front_terms(): pl.pallas_call(front_kernel, grid=(5,), out_shape=(jax.ShapeDtypeStruct((...  6.72 us
  transfers between devices with their start and end apart: 11, of which 4 were waited for; matrix products, arithmetic and copies ran while one was open for 4% of the time, Pallas kernels for 16%

profile of v3, /device:TPU:32, one launch (start us, length us, event | category | flops | bytes accessed | tf_op | source)
XLA Modules:
  0.0 158.2 jit_solution(16010975865917605379)
XLA Ops:
  7.2 0.7 all-gather.2.cloned.1.call-update
  7.9 1.8 %broadcast_in_dim.8 = bf16[4,32,2560]{2,1,0:T(8,128)(2,1)} broadcast(bf16[32,2560]{1,0:T(8,128)(2,1)} %param.6), dimensions={1,2} | broadcast | bytes 819200 | tf_op jit(solution)/shard_map/gathers/broadcast_in_dim | solution.py:62
  9.7 4.3 %all-to-all-start = ((bf16[4,32,2560]{2,1,0:T(8,128)(2,1)}), bf16[4,32,2560]{2,1,0:T(8,128)(2,1)S(1)}, u32[]{:S(2)}, u32[]{:S(2)}) async-start(bf16[4,32,2560]{2,1,0:T(8,128)(2,1)} %broadcast_in_dim.8), calls=%async_computation | async-start | bytes 1310720 | tf_op jit(solution)/shard_map/gathers/all_to_all | solution.py:63
  14.1 0.8 pad_maximum_fusion.q_ref
  15.4 1.3 fusion.5.slopes_ref
  16.7 6.7 %front_terms.1 = (f32[2560,128]{1,0:T(8,128)}, f32[128,128]{1,0:T(8,128)}, f32[128,128]{1,0:T(8,128)}) custom-call(s32[1]{0:T(128)} %bitcast.core_ref, bf16[992,2560]{1,0:T(8,128)(2,1)} %bitcast.40, bf16[992,256]{1,0:T(8,128)(2,1)} %fusion.5.slopes_ref, bf16[992,256]{1,0:T(8,128)(2,1)} %pad_maximum_fusion.q_ref), custom_call_target="tpu_custom_call" | custom-call | flops 1300234240 | bytes 7000000 | tf_op jit(solution)/shard_map/basis/front_terms/pallas_call | solution.py:98
  23.4 1.5 collective-permute-done.1.got_ref
  24.9 1.4 copy-done.2
  26.2 0.8 copy-done.4
  27.9 1.9 %collective-permute-done.2 = f32[1280,128]{1,0:T(8,128)S(1)} collective-permute-done((f32[1280,128]{1,0:T(8,128)S(1)}, f32[1280,128]{1,0:T(8,128)S(1)}, u32[]{:S(2)}, u32[]{:S(2)}) %collective-permute-start.2) | collective-permute-done | bytes 655392 | tf_op jit(solution)/shard_map/basis/ppermute | solution.py:397
  29.9 20.7 %all_to_all.30 = f32[16,80,128]{2,1,0:T(8,128)S(1)} all-to-all(f32[16,80,128]{2,1,0:T(8,128)S(1)} %bitcast.53), channel_id=1, replica_groups={{0,2,4,6,64,66,68,70,128,130,132,134,192,194,196,198},{1,3,5,7,65,67,69..., dimensions={0} | all-to-all | bytes 1310720 | tf_op jit(solution)/shard_map/basis/all_to_all | solution.py:398
  50.7 20.3 %all_to_all.31 = f32[8,80,128]{2,1,0:T(8,128)S(1)} all-to-all(f32[8,80,128]{2,1,0:T(8,128)S(1)} %broadcast_in_dim.9), channel_id=1, replica_groups={{0,8,16,24,32,40,48,56},{64,72,80,88,96,104,112,120},{128,136,144,152,1..., dimensions={0} | all-to-all | bytes 655360 | tf_op jit(solution)/shard_map/basis/all_to_all | solution.py:63
  71.1 14.0 %all_to_all.32 = f32[16,80,128]{2,1,0:T(8,128)S(1)} all-to-all(f32[16,80,128]{2,1,0:T(8,128)S(1)} %broadcast_in_dim.10), channel_id=1, replica_groups={{0,2,4,6,64,66,68,70,128,130,132,134,192,194,196,198},{1,3,5,7,65,67,69..., dimensions={0} | all-to-all | bytes 1310720 | tf_op jit(solution)/shard_map/basis/all_to_all | solution.py:63
  85.6 1.6 %collective-permute-done.3.other_ref = f32[1280,128]{1,0:T(8,128)S(1)} collective-permute-done((f32[1280,128]{1,0:T(8,128)S(1)}, f32[1280,128]{1,0:T(8,128)S(1)}, u32[]{:S(2)}, u32[]{:S(2)}) %collective-permute-start.3) | collective-permute-done | bytes 655392 | tf_op jit(solution)/shard_map/ppermute | solution.py:404
  87.2 7.2 %orthonormal.1.p_ref = bf16[2560,256]{1,0:T(8,128)(2,1)S(1)} custom-call(s32[1]{0:T(128)} %bitcast.core_ref, f32[1280,128]{1,0:T(8,128)S(1)} %bitcast.50, f32[1280,128]{1,0:T(8,128)S(1)} %collective-permute-done.3.other_ref), custom_call_target="tpu_custom_call" | custom-call | flops 2000000000 | bytes 4000000 | tf_op jit(solution)/shard_map/orthonormal/pallas_call | solution.py:210
  94.5 2.9 %factor_terms.1 = (bf16[1024,128]{1,0:T(8,128)(2,1)S(1)}, bf16[256,2560]{1,0:T(8,128)(2,1)S(1)}, bf16[256,2560]{1,0:T(8,128)(2,1)S(1)}) custom-call(s32[1]{0:T(128)} %bitcast.core_ref, bf16[992,2560]{1,0:T(8,128)(2,1)S(1)} %bitcast.44, bf16[992,256]{1,0:T(8,128)(2,1)S(1)} %copy-done, bf16[128,2560]{1,0:T(8,128)(2,1)S(1)} %bitcast.47, ...), custom_call_target="tpu_custom_call" | custom-call | flops 1342177280 | bytes 8000000 | tf_op jit(solution)/shard_map/right_factor/factor_terms/pallas_call | solution.py:248
  97.4 1.1 copy-done.5
  98.4 1.1 copy-done.6
  99.5 18.7 %all_to_all.33.blocks_ref = bf16[32,32,128]{2,1,0:T(8,128)(2,1)S(1)} all-to-all(bf16[32,32,128]{2,1,0:T(8,128)(2,1)S(1)} %bitcast.48), channel_id=1, replica_groups=mesh['replica'=32,'tensor'=8] {'replica'}, dimensions={0} | all-to-all | bytes 524288 | tf_op jit(solution)/shard_map/right_factor/all_to_all | solution.py:407
  118.2 0.8 mean_copies.1.order_ref
  119.0 2.5 %copy-done.1 = bf16[2560,992]{1,0:T(8,128)(2,1)S(1)} copy-done((bf16[2560,992]{1,0:T(8,128)(2,1)S(1)}, bf16[2560,992]{1,0:T(8,128)(2,1)}, u32[]{:S(2)}) %copy-start.1) | copy-done | bytes 5079064
  121.5 2.8 %grad_terms.1 = (f32[128,2560]{1,0:T(8,128)S(1)}, f32[128,2560]{1,0:T(8,128)S(1)}) custom-call(s32[1]{0:T(128)} %bitcast.core_ref, bf16[992,256]{1,0:T(8,128)(2,1)S(1)} %copy-done, bf16[2560,992]{1,0:T(8,128)(2,1)S(1)} %copy-done.1, bf16[1024,128]{1,0:T(8,128)(2,1)S(1)} %get-tuple-element.20.order_ref), custom_call_target="tpu_custom_call" | custom-call | flops 1300234240 | bytes 8000000 | tf_op jit(solution)/shard_map/input_grad/grad_terms/pallas_call | solution.py:349
  124.3 1.0 copy-done.3
  125.3 4.6 %all-to-all-start.5 = ((bf16[32,32,128]{2,1,0:T(8,128)(2,1)}), bf16[32,32,128]{2,1,0:T(8,128)(2,1)S(1)}, u32[]{:S(2)}, u32[]{:S(2)}) async-start(bf16[32,32,128]{2,1,0:T(8,128)(2,1)} %mean_copies.1.order_ref), calls=%async_computation.5 | async-start | bytes 524288 | tf_op jit(solution)/shard_map/right_factor/all_to_all | solution.py:409
  130.0 1.5 add.68
  131.5 1.1 collective-permute-start.5
  132.7 2.2 %collective-permute-start.7 = (bf16[32,2560]{1,0:T(8,128)(2,1)S(1)}, bf16[32,2560]{1,0:T(8,128)(2,1)S(1)}, u32[]{:S(2)}, u32[]{:S(2)}) collective-permute-start(bf16[32,2560]{1,0:T(8,128)(2,1)S(1)} %get-tuple-element.28), channel_id=1, source_target_pairs={{0,6},{1,7},{2,0},{3,1},{4,2},{5,3},{6,4},{7,5},{8,14},{9,15},{10,... | collective-permute-start | bytes 491528 | tf_op jit(solution)/shard_map/input_grad/ppermute | solution.py:378
  134.9 1.2 collective-permute-start.6
  136.1 6.7 %all-to-all-done.5 = bf16[32,32,128]{2,1,0:T(8,128)(2,1)S(1)} async-done(((bf16[32,32,128]{2,1,0:T(8,128)(2,1)}), bf16[32,32,128]{2,1,0:T(8,128)(2,1)S(1)}, u32[]{:S(2)}, u32[]{:S(2)}) %all-to-all-start.5) | async-done | bytes 262176 | tf_op jit(solution)/shard_map/right_factor/all_to_all | solution.py:409
  142.8 0.7 copy-done.10
  143.5 7.1 %residual.1 = (bf16[992,2560]{1,0:T(8,128)(2,1)}, f32[992,128]{1,0:T(8,128)}) custom-call(bf16[992,2560]{1,0:T(8,128)(2,1)} %bitcast.41, bf16[992,256]{1,0:T(8,128)(2,1)} %fusion.5.slopes_ref, bf16[256,2560]{1,0:T(8,128)(2,1)} %copy-done.6, bf16[256,2560]{1,0:T(8,128)(2,1)} %copy-done.5, bf16[1024,128]{1,0:T(8,128)(2,1)} %bitcast.54), custom_call_target="tpu_custom_call" | custom-call | flops 2684354560 | bytes 12000000 | tf_op jit(solution)/shard_map/residual/pallas_call | solution.py:293
  150.6 0.7 fusion.12
  (43 shorter events, 2.2 us)
Async XLA Ops:
  7.2 6.8 %copy-start.9 = (f32[992,128]{1,0:T(8,128)S(1)}, f32[992,128]{1,0:T(8,128)}, u32[]{:S(2)}) copy-start(f32[992,128]{1,0:T(8,128)} %param.11) | copy-start | bytes 1523716
  7.2 111.8 %all-gather.2.cloned.1.call-start = ((), (), s32[]{:S(2)}) async-start(), calls=%async_computation.6 | async-start | bytes 5406720 | tf_op jit(solution)/shard_map/gathers/all_gather | solution.py:388
  9.7 15.2 %all-to-all-start = ((bf16[4,32,2560]{2,1,0:T(8,128)(2,1)}), bf16[4,32,2560]{2,1,0:T(8,128)(2,1)S(1)}, u32[]{:S(2)}, u32[]{:S(2)}) async-start(bf16[4,32,2560]{2,1,0:T(8,128)(2,1)} %broadcast_in_dim.8), calls=%async_computation | async-start | bytes 1310720 | tf_op jit(solution)/shard_map/gathers/all_to_all | solution.py:63
  14.0 1.0 copy-start.7
  14.0 1.4 copy-start.8
  23.4 1.5 collective-permute-start.1
  24.9 1.4 copy-start.2
  26.2 0.8 copy-start.4
  27.6 2.2 %collective-permute-start.2 = (f32[1280,128]{1,0:T(8,128)S(1)}, f32[1280,128]{1,0:T(8,128)S(1)}, u32[]{:S(2)}, u32[]{:S(2)}) collective-permute-start(f32[1280,128]{1,0:T(8,128)S(1)} %get-tuple-element.19), channel_id=1, source_target_pairs={{0,1},{1,0},{2,3},{3,2},{4,5},{5,4},{6,7},{7,6},{8,9},{9,8},{10,11... | collective-permute-start | bytes 1966088 | tf_op jit(solution)/shard_map/basis/ppermute | solution.py:397
  29.8 64.6 %slice-start = ((s8[5079040]{0:T(1024)(128)(4,1)}), s8[884736]{0:T(1024)(128)(4,1)S(1)}, s32[]{:S(2)}) async-start(s8[5079040]{0:T(1024)(128)(4,1)} %bitcast.42), calls=%async_computation.7 | async-start | bytes 1769472
  71.1 23.3 %slice-start.1 = ((s8[5079040]{0:T(1024)(128)(4,1)}), s8[4194304]{0:T(1024)(128)(4,1)S(1)}, s32[]{:S(2)}) async-start(s8[5079040]{0:T(1024)(128)(4,1)} %bitcast.42), calls=%async_computation.8 | async-start | bytes 8388608
  85.1 9.4 %copy-start = (bf16[992,256]{1,0:T(8,128)(2,1)S(1)}, bf16[992,256]{1,0:T(8,128)(2,1)}, u32[]{:S(2)}) copy-start(bf16[992,256]{1,0:T(8,128)(2,1)} %fusion.5.slopes_ref) | copy-start | bytes 1523716
  85.1 2.1 %collective-permute-start.3 = (f32[1280,128]{1,0:T(8,128)S(1)}, f32[1280,128]{1,0:T(8,128)S(1)}, u32[]{:S(2)}, u32[]{:S(2)}) collective-permute-start(f32[1280,128]{1,0:T(8,128)S(1)} %bitcast.49), channel_id=1, source_target_pairs={{0,1},{1,0},{2,3},{3,2},{4,5},{5,4},{6,7},{7,6},{8,9},{9,8},{10,11... | collective-permute-start | bytes 1966088 | tf_op jit(solution)/shard_map/ppermute | solution.py:404
  85.1 9.3 %collective-permute-start = (bf16[128,2560]{1,0:T(8,128)(2,1)S(1)}, bf16[128,2560]{1,0:T(8,128)(2,1)S(1)}, u32[]{:S(2)}, u32[]{:S(2)}) collective-permute-start(bf16[128,2560]{1,0:T(8,128)(2,1)S(1)} %bitcast.46), channel_id=1, source_target_pairs={{0,1},{1,0},{2,3},{3,2},{4,5},{5,4},{6,7},{7,6},{8,9},{9,8},{10,11... | collective-permute-start | bytes 1966088 | tf_op jit(solution)/shard_map/gathers/ppermute | solution.py:391
  97.4 1.1 copy-start.5
  98.4 1.1 copy-start.6
  119.0 2.5 %copy-start.1 = (bf16[2560,992]{1,0:T(8,128)(2,1)S(1)}, bf16[2560,992]{1,0:T(8,128)(2,1)}, u32[]{:S(2)}) copy-start(bf16[2560,992]{1,0:T(8,128)(2,1)} %all-gather.2.cloned.1.call-done.weights_ref) | copy-start | bytes 15237124
  124.3 1.1 copy-start.3
  125.3 4.7 %collective-permute-start.4 = (f32[128,2560]{1,0:T(8,128)}, f32[128,2560]{1,0:T(8,128)}, u32[]{:S(2)}, u32[]{:S(2)}) collective-permute-start(f32[128,2560]{1,0:T(8,128)} %after.1), channel_id=1, source_target_pairs={{0,1},{1,0},{2,3},{3,2},{4,5},{5,4},{6,7},{7,6},{8,9},{9,8},{10,11... | collective-permute-start | bytes 3932168 | tf_op jit(solution)/shard_map/input_grad/ppermute | solution.py:413
  125.3 17.5 %all-to-all-start.5 = ((bf16[32,32,128]{2,1,0:T(8,128)(2,1)}), bf16[32,32,128]{2,1,0:T(8,128)(2,1)S(1)}, u32[]{:S(2)}, u32[]{:S(2)}) async-start(bf16[32,32,128]{2,1,0:T(8,128)(2,1)} %mean_copies.1.order_ref), calls=%async_computation.5 | async-start | bytes 524288 | tf_op jit(solution)/shard_map/right_factor/all_to_all | solution.py:409
  131.5 19.1 %collective-permute-start.5 = (bf16[32,2560]{1,0:T(8,128)(2,1)S(1)}, bf16[32,2560]{1,0:T(8,128)(2,1)S(1)}, u32[]{:S(2)}, u32[]{:S(2)}) collective-permute-start(bf16[32,2560]{1,0:T(8,128)(2,1)S(1)} %get-tuple-element.27), channel_id=1, source_target_pairs={{0,2},{1,3},{2,4},{3,5},{4,6},{5,7},{6,0},{7,1},{8,10},{9,11},{10,... | collective-permute-start | bytes 491528 | tf_op jit(solution)/shard_map/input_grad/ppermute | solution.py:378
  132.7 17.9 %collective-permute-start.7 = (bf16[32,2560]{1,0:T(8,128)(2,1)S(1)}, bf16[32,2560]{1,0:T(8,128)(2,1)S(1)}, u32[]{:S(2)}, u32[]{:S(2)}) collective-permute-start(bf16[32,2560]{1,0:T(8,128)(2,1)S(1)} %get-tuple-element.28), channel_id=1, source_target_pairs={{0,6},{1,7},{2,0},{3,1},{4,2},{5,3},{6,4},{7,5},{8,14},{9,15},{10,... | collective-permute-start | bytes 491528 | tf_op jit(solution)/shard_map/input_grad/ppermute | solution.py:378
  134.9 15.8 %collective-permute-start.6 = (bf16[32,2560]{1,0:T(8,128)(2,1)S(1)}, bf16[32,2560]{1,0:T(8,128)(2,1)S(1)}, u32[]{:S(2)}, u32[]{:S(2)}) collective-permute-start(bf16[32,2560]{1,0:T(8,128)(2,1)S(1)} %get-tuple-element.29), channel_id=1, source_target_pairs={{0,4},{1,5},{2,6},{3,7},{4,0},{5,1},{6,2},{7,3},{8,12},{9,13},{10,... | collective-permute-start | bytes 491528 | tf_op jit(solution)/shard_map/input_grad/ppermute | solution.py:378
  142.8 0.7 copy-start.10
Sparse Core Ops, SparseCore 0:
  10.6 94.6 all-gather.1

commit v4 on v3

--- a/solution.py
+++ b/solution.py
@@ -111,7 +111,7 @@
         ],
         out_specs=[pl.BlockSpec((512, RANK), lambda i: (i, 0)), here, here],
         scratch_shapes=[pltpu.VMEM((256, RANK), f32)],
-        compiler_params=pltpu.CompilerParams(vmem_limit_bytes=LARGE),
+        compiler_params=pltpu.CompilerParams(vmem_limit_bytes=20 * 2**20),
         cost_estimate=pl.CostEstimate(
             flops=2 * HIDDEN * DW * 256, bytes_accessed=7_000_000, transcendentals=0
         ),
@@ -225,7 +225,7 @@
 def factor_kernel(
     core_ref, error_ref, slopes_ref, mine_ref, other_ref, p_ref, *refs
 ):
-    out_ref, turned_ref, tokens_ref, y_ref = refs[-4:]
+    out_ref, tokens_ref, y_ref = refs[-3:]
     step = pl.program_id(0)
     core = core_ref[0]
 
@@ -237,7 +237,6 @@
                 tokens_ref[pl.ds(start, 32), :] = ref[32 * x : 32 * x + 32, :]
         y_ref[...] = split(folded(dot(tokens_ref[...], p_ref[...], 1, 0)))
 
-    turned_ref[...] = p_ref[pl.ds(pl.multiple_of(step * 640, 640), 640), :].T
     terms = dot(error_ref[...], p_ref[...], 1, 0) + dot(slopes_ref[...], y_ref[...], 1, 0)
     rows = lax.broadcasted_iota(jnp.int32, (TILE, RANK), 0) + step * TILE
     out_ref[...] = jnp.where(rows < HIDDEN, folded(terms), 0.0).astype(bf16)
@@ -250,8 +249,6 @@
         grid=(4,),
         out_shape=(
             jax.ShapeDtypeStruct((4 * TILE, RANK), bf16),
-            jax.ShapeDtypeStruct((2 * RANK, DW), bf16),
-            jax.ShapeDtypeStruct((256, DW), bf16),
         ),
         in_specs=[
             pl.BlockSpec(memory_space=pltpu.SMEM),
@@ -264,10 +261,8 @@
         + [pl.BlockSpec(memory_space=pl.ANY)] * len(order),
         out_specs=(
             pl.BlockSpec((TILE, RANK), lambda i: (i, 0)),
-            pl.BlockSpec((2 * RANK, 640), lambda i: (0, i)),
-            here,
-        ),
-        scratch_shapes=[pltpu.VMEM((256, 2 * RANK), bf16)],
+        ),
+        scratch_shapes=[pltpu.VMEM((256, DW), bf16), pltpu.VMEM((256, 2 * RANK), bf16)],
         compiler_params=pltpu.CompilerParams(vmem_limit_bytes=20 * 2**20),
         cost_estimate=pl.CostEstimate(
             flops=2 * 1024 * DW * 256, bytes_accessed=8_000_000, transcendentals=0
@@ -276,7 +271,38 @@
     )(core, error, slopes, mine, other, p_both, *order)
 
 
-def residual_kernel(error_ref, slopes_ref, tokens_ref, turned_ref, q_ref, out_ref, factor_ref):
+def turn_kernel(p_ref, order_ref, out_ref):
+    del order_ref
+    out_ref[...] = p_ref[...].T
+
+
+def turned_after(p_both, order):
+    here = pl.BlockSpec(memory_space=pltpu.VMEM)
+    return pl.pallas_call(
+        turn_kernel,
+        out_shape=jax.ShapeDtypeStruct((2 * RANK, DW), bf16),
+        in_specs=[here, pl.BlockSpec(memory_space=pl.ANY)],
+        out_specs=here,
+        compiler_params=pltpu.CompilerParams(vmem_limit_bytes=8 * 2**20),
+        cost_estimate=pl.CostEstimate(
+            flops=1_000_000, bytes_accessed=20_000_000, transcendentals=0
+        ),
+        name="turned_after",
+    )(p_both, order)
+
+
+def residual_kernel(
+    core_ref, error_ref, slopes_ref, mine_ref, other_ref, turned_ref, q_ref, out_ref, factor_ref, tokens_ref
+):
+    core = core_ref[0]
+
+    @pl.when(pl.program_id(0) == 0)
+    def _():
+        for x in range(4):
+            for ref, owner in ((mine_ref, core), (other_ref, 1 - core)):
+                start = pl.multiple_of((2 * x + owner) * 32, 32)
+                tokens_ref[pl.ds(start, 32), :] = ref[32 * x : 32 * x + 32, :]
+
     q = q_ref[...]
     factor_ref[...] = q.astype(f32)
     left = jnp.concatenate([slopes_ref[...], -q, -q], axis=1)
@@ -287,7 +313,7 @@
         out_ref[:, columns] = values.astype(bf16)
 
 
-def residual(error, slopes, tokens, turned, q_factor):
+def residual(core, error, slopes, mine, other, turned, q_factor):
     here = pl.BlockSpec(memory_space=pltpu.VMEM)
     rows = 496
     return pl.pallas_call(
@@ -298,8 +324,10 @@
             jax.ShapeDtypeStruct((HIDDEN, RANK), f32),
         ),
         in_specs=[
+            pl.BlockSpec(memory_space=pltpu.SMEM),
             pl.BlockSpec((rows, DW), lambda i: (i, 0)),
             pl.BlockSpec((rows, 256), lambda i: (i, 0)),
+            here,
             here,
             here,
             pl.BlockSpec((rows, RANK), lambda i: (i, 0)),
@@ -308,12 +336,13 @@
             pl.BlockSpec((rows, DW), lambda i: (i, 0)),
             pl.BlockSpec((rows, RANK), lambda i: (i, 0)),
         ],
+        scratch_shapes=[pltpu.VMEM((256, DW), bf16)],
         compiler_params=pltpu.CompilerParams(vmem_limit_bytes=LARGE),
         cost_estimate=pl.CostEstimate(
             flops=4 * 1024 * DW * 256, bytes_accessed=12_000_000, transcendentals=0
         ),
         name="residual",
-    )(error, slopes, tokens, turned, q_factor)
+    )(core, error, slopes, mine, other, turned, q_factor)
 
 
 def mean_kernel(blocks_ref, out_ref):
@@ -358,7 +387,7 @@
         ],
         out_specs=[pl.BlockSpec((128, width), lambda i: (0, i))] * 2,
         scratch_shapes=[pltpu.VMEM((256, width), f32)],
-        compiler_params=pltpu.CompilerParams(vmem_limit_bytes=16 * 2**20),
+        compiler_params=pltpu.CompilerParams(vmem_limit_bytes=LARGE - 9 * 2**18),
         cost_estimate=pl.CostEstimate(
             flops=2 * 256 * HIDDEN * DW, bytes_accessed=8_000_000, transcendentals=0
         ),
@@ -403,11 +432,12 @@
         half = broadcast_exchange(rows, 16, BOTH, XY_GROUPS).reshape(HALF, RANK)
     p_both = orthonormal(flag, half, lax.ppermute(half, "tensor", CORE_PAIRS))
     with jax.named_scope("right_factor"):
-        terms, turned, tokens = factor_terms(flag, error, slopes, mine, other, p_both)
+        (terms,) = factor_terms(flag, error, slopes, mine, other, p_both)
         blocks = lax.all_to_all(terms.reshape(32, 32, RANK), "replica", 0, 0)
         copies = mean_copies(blocks)
+        turned = turned_after(p_both, copies)
         q_block = lax.all_to_all(copies, "replica", 0, 0).reshape(1024, RANK)
-    error_out, q_factor = residual(error, slopes, tokens, turned, q_block)
+    error_out, q_factor = residual(flag, error, slopes, mine, other, turned, q_block)
     with jax.named_scope("input_grad"):
         own, pair = grad_terms(flag, slopes, weights, terms)
         own = own + lax.ppermute(after(pair, copies), "tensor", CORE_PAIRS)

time: 159 us -> 153 us (0.962)
  local copies, waits for them, and re-layouts: 10.9 us -> 8.09 us
  blocking collectives: 73.7 us -> 71.5 us
    pallas_call x1, Pallas kernels: 2.79 us -> 6.55 us  [grad_terms(): pl.pallas_call(grad_kernel, grid=(DW // width,), out_shape=(jax.ShapeDtyp...]
    pallas_call x1, Pallas kernels: 6.72 us -> 3.21 us  [front_terms(): pl.pallas_call(front_kernel, grid=(5,), out_shape=(jax.ShapeDtypeStruct((...]
    unnamed x26, local copies, waits for them, and re-layouts: 9.01 us -> 6.16 us
    all_to_all x1, waiting for transfers between devices: 0.01 us -> 2 us  [broadcast_exchange(): return lax.all_to_all(blocks, axis, 0, 0, axis_index_groups=groups)]
    all_to_all x1, blocking collectives: 20.7 us -> 18.7 us  [on_device(): lax.all_to_all(kept.reshape(16, HALF // 16, RANK), BOTH, 0, 0, axis_index...]
    all_to_all x1, waiting for transfers between devices: 6.73 us -> 4.91 us  [on_device(): q_block = lax.all_to_all(copies, 'replica', 0, 0).reshape(1024, RANK)]
  transfers between devices with their start and end apart: 11 -> 11, of which waited for: 4 -> 5; matrix products, arithmetic and copies ran while one was open for 4% -> 3% of each run, Pallas kernels for 16% -> 14%
where the time goes in v4:
time: 153 us
  blocking collectives  71.5 us (47%)
  Pallas kernels  28.7 us (19%)
  starting transfers between devices  14.5 us (9%)
  between operations  14.4 us (9%)
  waiting for transfers between devices  12.5 us (8%)
  local copies, waits for them, and re-layouts  8.09 us (5%)
  other arithmetic  3.02 us (2%)
    all_to_all x2, blocking collectives, broadcast_exchange(): return lax.all_to_all(blocks, axis, 0, 0, axis_index_groups=groups)  34.4 us
    all_to_all x1, blocking collectives, on_device(): lax.all_to_all(kept.reshape(16, HALF // 16, RANK), BOTH, 0, 0, axis_index...  18.7 us
    all_to_all x1, blocking collectives, on_device(): blocks = lax.all_to_all(terms.reshape(32, 32, RANK), 'replica', 0, 0)  18.4 us
    pallas_call x1, Pallas kernels, orthonormal(): pl.pallas_call(orthonormal_kernel, out_shape=jax.ShapeDtypeStruct((DW, 2...  7.22 us
    pallas_call x1, Pallas kernels, residual(): pl.pallas_call(residual_kernel, grid=(HIDDEN // rows,), out_shape=(jax.Sh...  7.17 us
    pallas_call x1, Pallas kernels, grad_terms(): pl.pallas_call(grad_kernel, grid=(DW // width,), out_shape=(jax.ShapeDtyp...  6.55 us
    unnamed x26, local copies, waits for them, and re-layouts  6.16 us
    all_to_all x1, waiting for transfers between devices, on_device(): q_block = lax.all_to_all(copies, 'replica', 0, 0).reshape(1024, RANK)  4.91 us
  transfers between devices with their start and end apart: 11, of which 5 were waited for; matrix products, arithmetic and copies ran while one was open for 3% of the time, Pallas kernels for 14%

profile of v4, /device:TPU:32, one launch (start us, length us, event | category | flops | bytes accessed | tf_op | source)
XLA Modules:
  0.0 152.8 jit_solution(4142925160817899956)
XLA Ops:
  7.2 0.7 all-gather.2.cloned.1.call-update
  7.9 1.8 %broadcast_in_dim.8 = bf16[4,32,2560]{2,1,0:T(8,128)(2,1)} broadcast(bf16[32,2560]{1,0:T(8,128)(2,1)} %param.6), dimensions={1,2} | broadcast | bytes 819200 | tf_op jit(solution)/shard_map/gathers/broadcast_in_dim | solution.py:62
  9.7 4.3 %all-to-all-start = ((bf16[4,32,2560]{2,1,0:T(8,128)(2,1)}), bf16[4,32,2560]{2,1,0:T(8,128)(2,1)S(1)}, u32[]{:S(2)}, u32[]{:S(2)}) async-start(bf16[4,32,2560]{2,1,0:T(8,128)(2,1)} %broadcast_in_dim.8), calls=%async_computation | async-start | bytes 1310720 | tf_op jit(solution)/shard_map/gathers/all_to_all | solution.py:63
  14.2 0.9 copy-done.7
  15.2 0.5 fusion.5.slopes_ref
  15.7 2.6 %copy-done = bf16[1,2560,992]{1,2,0:T(8,128)(2,1)S(1)} copy-done((bf16[1,2560,992]{1,2,0:T(8,128)(2,1)S(1)}, bf16[1,2560,992]{1,2,0:T(8,128)(2,1)}, u32[]{:S(2)}) %copy-start) | copy-done | bytes 5079064
  18.3 3.2 %front_terms.1 = (f32[2560,128]{1,0:T(8,128)S(1)}, f32[128,128]{1,0:T(8,128)S(1)}, f32[128,128]{1,0:T(8,128)S(1)}) custom-call(s32[1]{0:T(128)} %bitcast.core_ref, bf16[992,2560]{1,0:T(8,128)(2,1)S(1)} %bitcast.41, bf16[992,256]{1,0:T(8,128)(2,1)S(1)} %fusion.5.slopes_ref, bf16[992,256]{1,0:T(8,128)(2,1)S(1)} %pad_maximum_fusion.q_ref), custom_call_target="tpu_custom_call" | custom-call | flops 1300234240 | bytes 7000000 | tf_op jit(solution)/shard_map/basis/front_terms/pallas_call | solution.py:98
  21.6 1.2 collective-permute-done.1.got_ref
  22.9 2.0 %all-to-all-done = bf16[4,32,2560]{2,1,0:T(8,128)(2,1)S(1)} async-done(((bf16[4,32,2560]{2,1,0:T(8,128)(2,1)}), bf16[4,32,2560]{2,1,0:T(8,128)(2,1)S(1)}, u32[]{:S(2)}, u32[]{:S(2)}) %all-to-all-start) | async-done | bytes 655392 | tf_op jit(solution)/shard_map/gathers/all_to_all | solution.py:63
  24.9 0.5 left_terms.1
  25.5 2.1 %collective-permute-done.2 = f32[1280,128]{1,0:T(8,128)S(1)} collective-permute-done((f32[1280,128]{1,0:T(8,128)S(1)}, f32[1280,128]{1,0:T(8,128)S(1)}, u32[]{:S(2)}, u32[]{:S(2)}) %collective-permute-start.2) | collective-permute-done | bytes 655392 | tf_op jit(solution)/shard_map/basis/ppermute | solution.py:426
  27.7 18.7 %all_to_all.30 = f32[16,80,128]{2,1,0:T(8,128)S(1)} all-to-all(f32[16,80,128]{2,1,0:T(8,128)S(1)} %bitcast.54), channel_id=1, replica_groups={{0,2,4,6,64,66,68,70,128,130,132,134,192,194,196,198},{1,3,5,7,65,67,69..., dimensions={0} | all-to-all | bytes 1310720 | tf_op jit(solution)/shard_map/basis/all_to_all | solution.py:427
  46.5 19.4 %all_to_all.31 = f32[8,80,128]{2,1,0:T(8,128)S(1)} all-to-all(f32[8,80,128]{2,1,0:T(8,128)S(1)} %broadcast_in_dim.9), channel_id=1, replica_groups={{0,8,16,24,32,40,48,56},{64,72,80,88,96,104,112,120},{128,136,144,152,1..., dimensions={0} | all-to-all | bytes 655360 | tf_op jit(solution)/shard_map/basis/all_to_all | solution.py:63
  66.0 15.0 %all_to_all.32 = f32[16,80,128]{2,1,0:T(8,128)S(1)} all-to-all(f32[16,80,128]{2,1,0:T(8,128)S(1)} %broadcast_in_dim.10), channel_id=1, replica_groups={{0,2,4,6,64,66,68,70,128,130,132,134,192,194,196,198},{1,3,5,7,65,67,69..., dimensions={0} | all-to-all | bytes 1310720 | tf_op jit(solution)/shard_map/basis/all_to_all | solution.py:63
  81.0 0.5 collective-permute-start
  81.5 1.6 %collective-permute-done.3.other_ref = f32[1280,128]{1,0:T(8,128)S(1)} collective-permute-done((f32[1280,128]{1,0:T(8,128)S(1)}, f32[1280,128]{1,0:T(8,128)S(1)}, u32[]{:S(2)}, u32[]{:S(2)}) %collective-permute-start.3) | collective-permute-done | bytes 655392 | tf_op jit(solution)/shard_map/ppermute | solution.py:433
  83.1 7.2 %orthonormal.1.p_ref = bf16[2560,256]{1,0:T(8,128)(2,1)S(1)} custom-call(s32[1]{0:T(128)} %bitcast.core_ref, f32[1280,128]{1,0:T(8,128)S(1)} %bitcast.51, f32[1280,128]{1,0:T(8,128)S(1)} %collective-permute-done.3.other_ref), custom_call_target="tpu_custom_call" | custom-call | flops 2000000000 | bytes 4000000 | tf_op jit(solution)/shard_map/orthonormal/pallas_call | solution.py:210
  90.4 2.8 %factor_terms.1.order_ref = bf16[1024,128]{1,0:T(8,128)(2,1)S(1)} custom-call(s32[1]{0:T(128)} %bitcast.core_ref, bf16[992,2560]{1,0:T(8,128)(2,1)S(1)} %bitcast.44, bf16[992,256]{1,0:T(8,128)(2,1)S(1)} %fusion.5.slopes_ref, bf16[128,2560]{1,0:T(8,128)(2,1)S(1)} %bitcast.47, bf16[128,2560]{1,0:T(8,128)(2,1)S(1)} %collective-permute-done.other_ref, ...), custom_call_target="tpu_custom_call" | custom-call | flops 1342177280 | bytes 8000000 | tf_op jit(solution)/shard_map/right_factor/factor_terms/pallas_call | solution.py:247
  93.2 0.7 copy-done.3
  93.9 18.4 %all_to_all.33.blocks_ref = bf16[32,32,128]{2,1,0:T(8,128)(2,1)S(1)} all-to-all(bf16[32,32,128]{2,1,0:T(8,128)(2,1)S(1)} %bitcast.49), channel_id=1, replica_groups=mesh['replica'=32,'tensor'=8] {'replica'}, dimensions={0} | all-to-all | bytes 524288 | tf_op jit(solution)/shard_map/right_factor/all_to_all | solution.py:436
  112.3 0.8 mean_copies.1.order_ref
  113.1 6.6 %grad_terms.1 = (f32[128,2560]{1,0:T(8,128)}, f32[128,2560]{1,0:T(8,128)}) custom-call(s32[1]{0:T(128)} %bitcast.core_ref, bf16[992,256]{1,0:T(8,128)(2,1)} %copy-done.1, bf16[2560,992]{1,0:T(8,128)(2,1)} %all-gather.2.cloned.1.call-done.weights_ref, bf16[1024,128]{1,0:T(8,128)(2,1)} %copy-done.3), custom_call_target="tpu_custom_call" | custom-call | flops 1300234240 | bytes 8000000 | tf_op jit(solution)/shard_map/input_grad/grad_terms/pallas_call | solution.py:378
  119.7 4.7 %all-to-all-start.5 = ((bf16[32,32,128]{2,1,0:T(8,128)(2,1)}), bf16[32,32,128]{2,1,0:T(8,128)(2,1)S(1)}, u32[]{:S(2)}, u32[]{:S(2)}) async-start(bf16[32,32,128]{2,1,0:T(8,128)(2,1)} %mean_copies.1.order_ref), calls=%async_computation.5 | async-start | bytes 524288 | tf_op jit(solution)/shard_map/right_factor/all_to_all | solution.py:439
  124.9 1.1 copy-done.4
  125.9 1.5 add.68
  127.5 1.6 %collective-permute-start.5 = (bf16[32,2560]{1,0:T(8,128)(2,1)S(1)}, bf16[32,2560]{1,0:T(8,128)(2,1)S(1)}, u32[]{:S(2)}, u32[]{:S(2)}) collective-permute-start(bf16[32,2560]{1,0:T(8,128)(2,1)S(1)} %get-tuple-element.21), channel_id=1, source_target_pairs={{0,2},{1,3},{2,4},{3,5},{4,6},{5,7},{6,0},{7,1},{8,10},{9,11},{10,... | collective-permute-start | bytes 491528 | tf_op jit(solution)/shard_map/input_grad/ppermute | solution.py:407
  129.1 1.7 %collective-permute-start.7 = (bf16[32,2560]{1,0:T(8,128)(2,1)S(1)}, bf16[32,2560]{1,0:T(8,128)(2,1)S(1)}, u32[]{:S(2)}, u32[]{:S(2)}) collective-permute-start(bf16[32,2560]{1,0:T(8,128)(2,1)S(1)} %get-tuple-element.22), channel_id=1, source_target_pairs={{0,6},{1,7},{2,0},{3,1},{4,2},{5,3},{6,4},{7,5},{8,14},{9,15},{10,... | collective-permute-start | bytes 491528 | tf_op jit(solution)/shard_map/input_grad/ppermute | solution.py:407
  130.8 1.5 collective-permute-start.6
  132.3 4.9 %all-to-all-done.5 = bf16[32,32,128]{2,1,0:T(8,128)(2,1)S(1)} async-done(((bf16[32,32,128]{2,1,0:T(8,128)(2,1)}), bf16[32,32,128]{2,1,0:T(8,128)(2,1)S(1)}, u32[]{:S(2)}, u32[]{:S(2)}) %all-to-all-start.5) | async-done | bytes 262176 | tf_op jit(solution)/shard_map/right_factor/all_to_all | solution.py:439
  137.3 0.7 copy-done.10
  138.0 7.2 %residual.1 = (bf16[992,2560]{1,0:T(8,128)(2,1)}, f32[992,128]{1,0:T(8,128)}) custom-call(s32[1]{0:T(128)} %bitcast.core_ref, bf16[992,2560]{1,0:T(8,128)(2,1)} %bitcast.40, bf16[992,256]{1,0:T(8,128)(2,1)} %copy-done.1, bf16[128,2560]{1,0:T(8,128)(2,1)} %bitcast.48, bf16[128,2560]{1,0:T(8,128)(2,1)} %copy-done.5, bf16[256,2560]{1,0:T(8,128)(2,1)} %copy-done.4, ...), custom_call_target="tpu_custom_call" | custom-call | flops 2684354560 | bytes 12000000 | tf_op jit(solution)/shard_map/residual/pallas_call | solution.py:319
  145.2 0.7 fusion.12
  (44 shorter events, 1.2 us)
Async XLA Ops:
  7.2 6.8 %copy-start.9 = (f32[992,128]{1,0:T(8,128)S(1)}, f32[992,128]{1,0:T(8,128)}, u32[]{:S(2)}) copy-start(f32[992,128]{1,0:T(8,128)} %param.11) | copy-start | bytes 1523716
  7.2 105.9 %all-gather.2.cloned.1.call-start = ((), (), s32[]{:S(2)}) async-start(), calls=%async_computation.6 | async-start | bytes 5406720 | tf_op jit(solution)/shard_map/gathers/all_gather | solution.py:417
  9.7 15.2 %all-to-all-start = ((bf16[4,32,2560]{2,1,0:T(8,128)(2,1)}), bf16[4,32,2560]{2,1,0:T(8,128)(2,1)S(1)}, u32[]{:S(2)}, u32[]{:S(2)}) async-start(bf16[4,32,2560]{2,1,0:T(8,128)(2,1)} %broadcast_in_dim.8), calls=%async_computation | async-start | bytes 1310720 | tf_op jit(solution)/shard_map/gathers/all_to_all | solution.py:63
  14.0 1.0 copy-start.7
  14.0 1.2 copy-start.8
  15.7 74.6 %copy-start.1 = (bf16[992,256]{1,0:T(8,128)(2,1)}, bf16[992,256]{1,0:T(8,128)(2,1)S(1)}, u32[]{:S(2)}) copy-start(bf16[992,256]{1,0:T(8,128)(2,1)S(1)} %fusion.5.slopes_ref) | copy-start | bytes 1523716
  15.7 2.6 %copy-start = (bf16[1,2560,992]{1,2,0:T(8,128)(2,1)S(1)}, bf16[1,2560,992]{1,2,0:T(8,128)(2,1)}, u32[]{:S(2)}) copy-start(bf16[1,2560,992]{1,2,0:T(8,128)(2,1)} %param.10) | copy-start | bytes 15237124
  21.5 1.3 collective-permute-start.1
  24.9 65.4 %copy-start.2 = (bf16[4,32,2560]{2,1,0:T(8,128)(2,1)}, bf16[4,32,2560]{2,1,0:T(8,128)(2,1)S(1)}, u32[]{:S(2)}) copy-start(bf16[4,32,2560]{2,1,0:T(8,128)(2,1)S(1)} %all-to-all-done) | copy-start | bytes 1966084
  25.4 2.2 %collective-permute-start.2 = (f32[1280,128]{1,0:T(8,128)S(1)}, f32[1280,128]{1,0:T(8,128)S(1)}, u32[]{:S(2)}, u32[]{:S(2)}) collective-permute-start(f32[1280,128]{1,0:T(8,128)S(1)} %get-tuple-element.16), channel_id=1, source_target_pairs={{0,1},{1,0},{2,3},{3,2},{4,5},{5,4},{6,7},{7,6},{8,9},{9,8},{10,11... | collective-permute-start | bytes 1966088 | tf_op jit(solution)/shard_map/basis/ppermute | solution.py:426
  27.6 62.7 %slice-start = ((s8[5079040]{0:T(1024)(128)(4,1)}), s8[884736]{0:T(1024)(128)(4,1)S(1)}, s32[]{:S(2)}) async-start(s8[5079040]{0:T(1024)(128)(4,1)} %bitcast.42), calls=%async_computation.7 | async-start | bytes 1769472
  66.0 24.3 %slice-start.1 = ((s8[5079040]{0:T(1024)(128)(4,1)}), s8[4194304]{0:T(1024)(128)(4,1)S(1)}, s32[]{:S(2)}) async-start(s8[5079040]{0:T(1024)(128)(4,1)} %bitcast.42), calls=%async_computation.8 | async-start | bytes 8388608
  81.0 2.1 %collective-permute-start.3 = (f32[1280,128]{1,0:T(8,128)S(1)}, f32[1280,128]{1,0:T(8,128)S(1)}, u32[]{:S(2)}, u32[]{:S(2)}) collective-permute-start(f32[1280,128]{1,0:T(8,128)S(1)} %bitcast.50), channel_id=1, source_target_pairs={{0,1},{1,0},{2,3},{3,2},{4,5},{5,4},{6,7},{7,6},{8,9},{9,8},{10,11... | collective-permute-start | bytes 1966088 | tf_op jit(solution)/shard_map/ppermute | solution.py:433
  81.0 9.3 %collective-permute-start = (bf16[128,2560]{1,0:T(8,128)(2,1)S(1)}, bf16[128,2560]{1,0:T(8,128)(2,1)S(1)}, u32[]{:S(2)}, u32[]{:S(2)}) collective-permute-start(bf16[128,2560]{1,0:T(8,128)(2,1)S(1)} %bitcast.46), channel_id=1, source_target_pairs={{0,1},{1,0},{2,3},{3,2},{4,5},{5,4},{6,7},{7,6},{8,9},{9,8},{10,11... | collective-permute-start | bytes 1966088 | tf_op jit(solution)/shard_map/gathers/ppermute | solution.py:420
  90.4 2.8 %copy-start.5 = (bf16[128,2560]{1,0:T(8,128)(2,1)}, bf16[128,2560]{1,0:T(8,128)(2,1)S(1)}, u32[]{:S(2)}) copy-start(bf16[128,2560]{1,0:T(8,128)(2,1)S(1)} %collective-permute-done.other_ref) | copy-start | bytes 1966084
  93.2 0.7 copy-start.3
  119.7 6.3 %collective-permute-start.4 = (f32[128,2560]{1,0:T(8,128)}, f32[128,2560]{1,0:T(8,128)}, u32[]{:S(2)}, u32[]{:S(2)}) collective-permute-start(f32[128,2560]{1,0:T(8,128)} %after.1), channel_id=1, source_target_pairs={{0,1},{1,0},{2,3},{3,2},{4,5},{5,4},{6,7},{7,6},{8,9},{9,8},{10,11... | collective-permute-start | bytes 3932168 | tf_op jit(solution)/shard_map/input_grad/ppermute | solution.py:443
  119.7 17.6 %all-to-all-start.5 = ((bf16[32,32,128]{2,1,0:T(8,128)(2,1)}), bf16[32,32,128]{2,1,0:T(8,128)(2,1)S(1)}, u32[]{:S(2)}, u32[]{:S(2)}) async-start(bf16[32,32,128]{2,1,0:T(8,128)(2,1)} %mean_copies.1.order_ref), calls=%async_computation.5 | async-start | bytes 524288 | tf_op jit(solution)/shard_map/right_factor/all_to_all | solution.py:439
  124.4 1.5 copy-start.6
  124.8 1.1 copy-start.4
  127.5 17.6 %collective-permute-start.5 = (bf16[32,2560]{1,0:T(8,128)(2,1)S(1)}, bf16[32,2560]{1,0:T(8,128)(2,1)S(1)}, u32[]{:S(2)}, u32[]{:S(2)}) collective-permute-start(bf16[32,2560]{1,0:T(8,128)(2,1)S(1)} %get-tuple-element.21), channel_id=1, source_target_pairs={{0,2},{1,3},{2,4},{3,5},{4,6},{5,7},{6,0},{7,1},{8,10},{9,11},{10,... | collective-permute-start | bytes 491528 | tf_op jit(solution)/shard_map/input_grad/ppermute | solution.py:407
  129.1 16.1 %collective-permute-start.7 = (bf16[32,2560]{1,0:T(8,128)(2,1)S(1)}, bf16[32,2560]{1,0:T(8,128)(2,1)S(1)}, u32[]{:S(2)}, u32[]{:S(2)}) collective-permute-start(bf16[32,2560]{1,0:T(8,128)(2,1)S(1)} %get-tuple-element.22), channel_id=1, source_target_pairs={{0,6},{1,7},{2,0},{3,1},{4,2},{5,3},{6,4},{7,5},{8,14},{9,15},{10,... | collective-permute-start | bytes 491528 | tf_op jit(solution)/shard_map/input_grad/ppermute | solution.py:407
  130.8 14.3 %collective-permute-start.6 = (bf16[32,2560]{1,0:T(8,128)(2,1)S(1)}, bf16[32,2560]{1,0:T(8,128)(2,1)S(1)}, u32[]{:S(2)}, u32[]{:S(2)}) collective-permute-start(bf16[32,2560]{1,0:T(8,128)(2,1)S(1)} %get-tuple-element.23), channel_id=1, source_target_pairs={{0,4},{1,5},{2,6},{3,7},{4,0},{5,1},{6,2},{7,3},{8,12},{9,13},{10,... | collective-permute-start | bytes 491528 | tf_op jit(solution)/shard_map/input_grad/ppermute | solution.py:407
  137.3 0.7 copy-start.10
Sparse Core Ops, SparseCore 0:
  10.6 97.3 all-gather.1

commit v5 on v4

--- a/solution.py
+++ b/solution.py
@@ -79,18 +79,21 @@
     )(values, order)
 
 
-def front_kernel(core_ref, error_ref, slopes_ref, q_ref, error_out_ref, own_ref, pair_ref, z_ref):
+def front_kernel(
+    core_ref, error_ref, slopes_ref, q_ref, error_out_ref, own_ref, pair_ref, z_ref, both_ref
+):
     core = core_ref[0]
 
     @pl.when(pl.program_id(0) == 0)
     def _():
-        z_ref[...] = folded(dot(slopes_ref[...], q_ref[...], 0, 0))
+        both_ref[...] = split(q_ref[...])
+        z_ref[...] = folded(dot(slopes_ref[...], both_ref[...], 0, 0))
         for x in range(4):
             for ref, owner in ((own_ref, core), (pair_ref, 1 - core)):
                 start = pl.multiple_of((2 * x + owner) * 32, 32)
                 ref[32 * x : 32 * x + 32, :] = z_ref[pl.ds(start, 32), :]
 
-    error_out_ref[...] = folded(dot(error_ref[...], q_ref[...], 0, 0))
+    error_out_ref[...] = folded(dot(error_ref[...], both_ref[...], 0, 0))
 
 
 def front_terms(core, error, slopes, q_both):
@@ -110,7 +113,7 @@
             here,
         ],
         out_specs=[pl.BlockSpec((512, RANK), lambda i: (i, 0)), here, here],
-        scratch_shapes=[pltpu.VMEM((256, RANK), f32)],
+        scratch_shapes=[pltpu.VMEM((256, RANK), f32), pltpu.VMEM((HIDDEN, 2 * RANK), bf16)],
         compiler_params=pltpu.CompilerParams(vmem_limit_bytes=20 * 2**20),
         cost_estimate=pl.CostEstimate(
             flops=2 * HIDDEN * DW * 256, bytes_accessed=7_000_000, transcendentals=0
@@ -419,8 +422,7 @@
         mine = broadcast_exchange(inputs, 4, "tensor", X_GROUPS).reshape(128, DW)
         other = lax.ppermute(mine, "tensor", CORE_PAIRS)
     with jax.named_scope("basis"):
-        q_both = split_outside(q_prev)
-        errors, own, pair = front_terms(flag, error, slopes, q_both)
+        errors, own, pair = front_terms(flag, error, slopes, q_prev)
         got = lax.ppermute(pair, "tensor", CORE_PAIRS)
         kept, sent = left_terms(flag, mine, own, got, errors)
         kept = kept + lax.ppermute(sent, "tensor", CORE_PAIRS)

time: 153 us -> 153 us (level)
  transfers between devices with their start and end apart: 11 -> 11, of which waited for: 5 -> 5; matrix products, arithmetic and copies ran while one was open for 3% -> 3% of each run, Pallas kernels for 14% -> 15%
where the time goes in v5:
time: 153 us
  blocking collectives  71.2 us (47%)
  Pallas kernels  28.7 us (19%)
  starting transfers between devices  14.7 us (10%)
  between operations  14.4 us (9%)
  waiting for transfers between devices  13.7 us (9%)
  local copies, waits for them, and re-layouts  7.05 us (5%)
  other arithmetic  2.88 us (2%)
    all_to_all x2, blocking collectives, broadcast_exchange(): return lax.all_to_all(blocks, axis, 0, 0, axis_index_groups=groups)  34.4 us
    all_to_all x1, blocking collectives, on_device(): blocks = lax.all_to_all(terms.reshape(32, 32, RANK), 'replica', 0, 0)  18.4 us
    all_to_all x1, blocking collectives, on_device(): lax.all_to_all(kept.reshape(16, HALF // 16, RANK), BOTH, 0, 0, axis_index...  18.4 us
    pallas_call x1, Pallas kernels, orthonormal(): pl.pallas_call(orthonormal_kernel, out_shape=jax.ShapeDtypeStruct((DW, 2...  7.22 us
    pallas_call x1, Pallas kernels, residual(): pl.pallas_call(residual_kernel, grid=(HIDDEN // rows,), out_shape=(jax.Sh...  7.18 us
    pallas_call x1, Pallas kernels, grad_terms(): pl.pallas_call(grad_kernel, grid=(DW // width,), out_shape=(jax.ShapeDtyp...  6.55 us
    unnamed x26, local copies, waits for them, and re-layouts  5.13 us
    all_to_all x1, waiting for transfers between devices, on_device(): q_block = lax.all_to_all(copies, 'replica', 0, 0).reshape(1024, RANK)  4.96 us
  transfers between devices with their start and end apart: 11, of which 5 were waited for; matrix products, arithmetic and copies ran while one was open for 3% of the time, Pallas kernels for 15%

profile of v5, /device:TPU:32, one launch (start us, length us, event | category | flops | bytes accessed | tf_op | source)
XLA Modules:
  0.0 152.7 jit_solution(9626948914436582791)
XLA Ops:
  7.2 0.7 all-gather.2.cloned.1.call-update
  7.9 1.8 %broadcast_in_dim.8 = bf16[4,32,2560]{2,1,0:T(8,128)(2,1)} broadcast(bf16[32,2560]{1,0:T(8,128)(2,1)} %param.6), dimensions={1,2} | broadcast | bytes 819200 | tf_op jit(solution)/shard_map/gathers/broadcast_in_dim | solution.py:62
  9.7 4.4 %all-to-all-start = ((bf16[4,32,2560]{2,1,0:T(8,128)(2,1)}), bf16[4,32,2560]{2,1,0:T(8,128)(2,1)S(1)}, u32[]{:S(2)}, u32[]{:S(2)}) async-start(bf16[4,32,2560]{2,1,0:T(8,128)(2,1)} %broadcast_in_dim.8), calls=%async_computation | async-start | bytes 1310720 | tf_op jit(solution)/shard_map/gathers/all_to_all | solution.py:63
  14.1 0.5 fusion.5.slopes_ref
  14.7 2.6 %copy-done = bf16[1,2560,992]{1,2,0:T(8,128)(2,1)S(1)} copy-done((bf16[1,2560,992]{1,2,0:T(8,128)(2,1)S(1)}, bf16[1,2560,992]{1,2,0:T(8,128)(2,1)}, u32[]{:S(2)}) %copy-start) | copy-done | bytes 5079064
  17.3 3.2 %front_terms.1 = (f32[2560,128]{1,0:T(8,128)S(1)}, f32[128,128]{1,0:T(8,128)S(1)}, f32[128,128]{1,0:T(8,128)S(1)}) custom-call(s32[1]{0:T(128)} %bitcast.core_ref, bf16[992,2560]{1,0:T(8,128)(2,1)S(1)} %bitcast.41, bf16[992,256]{1,0:T(8,128)(2,1)S(1)} %fusion.5.slopes_ref, f32[992,128]{1,0:T(8,128)S(1)} %copy-done.6), custom_call_target="tpu_custom_call" | custom-call | flops 1300234240 | bytes 7000000 | tf_op jit(solution)/shard_map/basis/front_terms/pallas_call | solution.py:101
  20.6 1.2 collective-permute-done.1.got_ref
  21.8 3.2 %all-to-all-done = bf16[4,32,2560]{2,1,0:T(8,128)(2,1)S(1)} async-done(((bf16[4,32,2560]{2,1,0:T(8,128)(2,1)}), bf16[4,32,2560]{2,1,0:T(8,128)(2,1)S(1)}, u32[]{:S(2)}, u32[]{:S(2)}) %all-to-all-start) | async-done | bytes 655392 | tf_op jit(solution)/shard_map/gathers/all_to_all | solution.py:63
  25.0 0.5 left_terms.1
  25.7 2.1 %collective-permute-done.2 = f32[1280,128]{1,0:T(8,128)S(1)} collective-permute-done((f32[1280,128]{1,0:T(8,128)S(1)}, f32[1280,128]{1,0:T(8,128)S(1)}, u32[]{:S(2)}, u32[]{:S(2)}) %collective-permute-start.2) | collective-permute-done | bytes 655392 | tf_op jit(solution)/shard_map/basis/ppermute | solution.py:428
  27.8 18.4 %all_to_all.30 = f32[16,80,128]{2,1,0:T(8,128)S(1)} all-to-all(f32[16,80,128]{2,1,0:T(8,128)S(1)} %bitcast.54), channel_id=1, replica_groups={{0,2,4,6,64,66,68,70,128,130,132,134,192,194,196,198},{1,3,5,7,65,67,69..., dimensions={0} | all-to-all | bytes 1310720 | tf_op jit(solution)/shard_map/basis/all_to_all | solution.py:429
  46.3 19.4 %all_to_all.31 = f32[8,80,128]{2,1,0:T(8,128)S(1)} all-to-all(f32[8,80,128]{2,1,0:T(8,128)S(1)} %broadcast_in_dim.9), channel_id=1, replica_groups={{0,8,16,24,32,40,48,56},{64,72,80,88,96,104,112,120},{128,136,144,152,1..., dimensions={0} | all-to-all | bytes 655360 | tf_op jit(solution)/shard_map/basis/all_to_all | solution.py:63
  65.8 15.1 %all_to_all.32 = f32[16,80,128]{2,1,0:T(8,128)S(1)} all-to-all(f32[16,80,128]{2,1,0:T(8,128)S(1)} %broadcast_in_dim.10), channel_id=1, replica_groups={{0,2,4,6,64,66,68,70,128,130,132,134,192,194,196,198},{1,3,5,7,65,67,69..., dimensions={0} | all-to-all | bytes 1310720 | tf_op jit(solution)/shard_map/basis/all_to_all | solution.py:63
  80.8 0.5 collective-permute-start
  81.3 1.6 %collective-permute-done.3.other_ref = f32[1280,128]{1,0:T(8,128)S(1)} collective-permute-done((f32[1280,128]{1,0:T(8,128)S(1)}, f32[1280,128]{1,0:T(8,128)S(1)}, u32[]{:S(2)}, u32[]{:S(2)}) %collective-permute-start.3) | collective-permute-done | bytes 655392 | tf_op jit(solution)/shard_map/ppermute | solution.py:435
  82.9 7.2 %orthonormal.1.p_ref = bf16[2560,256]{1,0:T(8,128)(2,1)S(1)} custom-call(s32[1]{0:T(128)} %bitcast.core_ref, f32[1280,128]{1,0:T(8,128)S(1)} %bitcast.51, f32[1280,128]{1,0:T(8,128)S(1)} %collective-permute-done.3.other_ref), custom_call_target="tpu_custom_call" | custom-call | flops 2000000000 | bytes 4000000 | tf_op jit(solution)/shard_map/orthonormal/pallas_call | solution.py:213
  90.2 2.8 %factor_terms.1.order_ref = bf16[1024,128]{1,0:T(8,128)(2,1)S(1)} custom-call(s32[1]{0:T(128)} %bitcast.core_ref, bf16[992,2560]{1,0:T(8,128)(2,1)S(1)} %bitcast.44, bf16[992,256]{1,0:T(8,128)(2,1)S(1)} %fusion.5.slopes_ref, bf16[128,2560]{1,0:T(8,128)(2,1)S(1)} %bitcast.47, bf16[128,2560]{1,0:T(8,128)(2,1)S(1)} %collective-permute-done.other_ref, ...), custom_call_target="tpu_custom_call" | custom-call | flops 1342177280 | bytes 8000000 | tf_op jit(solution)/shard_map/right_factor/factor_terms/pallas_call | solution.py:250
  93.0 0.7 copy-done.3
  93.7 18.4 %all_to_all.33.blocks_ref = bf16[32,32,128]{2,1,0:T(8,128)(2,1)S(1)} all-to-all(bf16[32,32,128]{2,1,0:T(8,128)(2,1)S(1)} %bitcast.49), channel_id=1, replica_groups=mesh['replica'=32,'tensor'=8] {'replica'}, dimensions={0} | all-to-all | bytes 524288 | tf_op jit(solution)/shard_map/right_factor/all_to_all | solution.py:438
  112.1 0.8 mean_copies.1.order_ref
  112.9 6.6 %grad_terms.1 = (f32[128,2560]{1,0:T(8,128)}, f32[128,2560]{1,0:T(8,128)}) custom-call(s32[1]{0:T(128)} %bitcast.core_ref, bf16[992,256]{1,0:T(8,128)(2,1)} %copy-done.1, bf16[2560,992]{1,0:T(8,128)(2,1)} %all-gather.2.cloned.1.call-done.weights_ref, bf16[1024,128]{1,0:T(8,128)(2,1)} %copy-done.3), custom_call_target="tpu_custom_call" | custom-call | flops 1300234240 | bytes 8000000 | tf_op jit(solution)/shard_map/input_grad/grad_terms/pallas_call | solution.py:381
  119.5 4.8 %all-to-all-start.5 = ((bf16[32,32,128]{2,1,0:T(8,128)(2,1)}), bf16[32,32,128]{2,1,0:T(8,128)(2,1)S(1)}, u32[]{:S(2)}, u32[]{:S(2)}) async-start(bf16[32,32,128]{2,1,0:T(8,128)(2,1)} %mean_copies.1.order_ref), calls=%async_computation.5 | async-start | bytes 524288 | tf_op jit(solution)/shard_map/right_factor/all_to_all | solution.py:441
  124.4 0.4 turned_after.1.turned_ref
  124.8 1.1 copy-done.4
  125.9 1.5 add.68
  127.4 1.4 collective-permute-start.5
  128.8 1.9 %collective-permute-start.7 = (bf16[32,2560]{1,0:T(8,128)(2,1)S(1)}, bf16[32,2560]{1,0:T(8,128)(2,1)S(1)}, u32[]{:S(2)}, u32[]{:S(2)}) collective-permute-start(bf16[32,2560]{1,0:T(8,128)(2,1)S(1)} %get-tuple-element.22), channel_id=1, source_target_pairs={{0,6},{1,7},{2,0},{3,1},{4,2},{5,3},{6,4},{7,5},{8,14},{9,15},{10,... | collective-permute-start | bytes 491528 | tf_op jit(solution)/shard_map/input_grad/ppermute | solution.py:410
  130.8 1.5 collective-permute-start.6
  132.2 5.0 %all-to-all-done.5 = bf16[32,32,128]{2,1,0:T(8,128)(2,1)S(1)} async-done(((bf16[32,32,128]{2,1,0:T(8,128)(2,1)}), bf16[32,32,128]{2,1,0:T(8,128)(2,1)S(1)}, u32[]{:S(2)}, u32[]{:S(2)}) %all-to-all-start.5) | async-done | bytes 262176 | tf_op jit(solution)/shard_map/right_factor/all_to_all | solution.py:441
  137.2 0.7 copy-done.10
  137.9 7.2 %residual.1 = (bf16[992,2560]{1,0:T(8,128)(2,1)}, f32[992,128]{1,0:T(8,128)}) custom-call(s32[1]{0:T(128)} %bitcast.core_ref, bf16[992,2560]{1,0:T(8,128)(2,1)} %bitcast.40, bf16[992,256]{1,0:T(8,128)(2,1)} %copy-done.1, bf16[128,2560]{1,0:T(8,128)(2,1)} %bitcast.48, bf16[128,2560]{1,0:T(8,128)(2,1)} %copy-done.5, bf16[256,2560]{1,0:T(8,128)(2,1)} %copy-done.4, ...), custom_call_target="tpu_custom_call" | custom-call | flops 2684354560 | bytes 12000000 | tf_op jit(solution)/shard_map/residual/pallas_call | solution.py:322
  145.1 0.7 fusion.11
  (42 shorter events, 0.6 us)
Async XLA Ops:
  7.2 7.0 %copy-start.9 = (bf16[256,992]{0,1:T(8,128)(2,1)S(1)}, bf16[256,992]{0,1:T(8,128)(2,1)}, u32[]{:S(2)}) copy-start(bf16[256,992]{0,1:T(8,128)(2,1)} %param.8) | copy-start | bytes 1523716
  7.2 7.0 %copy-start.8 = (bf16[256,992]{0,1:T(8,128)(2,1)S(1)}, bf16[256,992]{0,1:T(8,128)(2,1)}, u32[]{:S(2)}) copy-start(bf16[256,992]{0,1:T(8,128)(2,1)} %param.7) | copy-start | bytes 1523716
  7.2 105.7 %all-gather.2.cloned.1.call-start = ((), (), s32[]{:S(2)}) async-start(), calls=%async_computation.6 | async-start | bytes 5406720 | tf_op jit(solution)/shard_map/gathers/all_gather | solution.py:420
  9.7 4.9 %copy-start.6 = (f32[992,128]{1,0:T(8,128)S(1)}, f32[992,128]{1,0:T(8,128)}, u32[]{:S(2)}) copy-start(f32[992,128]{1,0:T(8,128)} %q_ref.1) | copy-start | bytes 1523716
  9.7 15.3 %all-to-all-start = ((bf16[4,32,2560]{2,1,0:T(8,128)(2,1)}), bf16[4,32,2560]{2,1,0:T(8,128)(2,1)S(1)}, u32[]{:S(2)}, u32[]{:S(2)}) async-start(bf16[4,32,2560]{2,1,0:T(8,128)(2,1)} %broadcast_in_dim.8), calls=%async_computation | async-start | bytes 1310720 | tf_op jit(solution)/shard_map/gathers/all_to_all | solution.py:63
  14.6 75.5 %copy-start.1 = (bf16[992,256]{1,0:T(8,128)(2,1)}, bf16[992,256]{1,0:T(8,128)(2,1)S(1)}, u32[]{:S(2)}) copy-start(bf16[992,256]{1,0:T(8,128)(2,1)S(1)} %fusion.5.slopes_ref) | copy-start | bytes 1523716
  14.7 2.6 %copy-start = (bf16[1,2560,992]{1,2,0:T(8,128)(2,1)S(1)}, bf16[1,2560,992]{1,2,0:T(8,128)(2,1)}, u32[]{:S(2)}) copy-start(bf16[1,2560,992]{1,2,0:T(8,128)(2,1)} %param.10) | copy-start | bytes 15237124
  20.5 1.3 collective-permute-start.1
  25.0 65.1 %copy-start.2 = (bf16[4,32,2560]{2,1,0:T(8,128)(2,1)}, bf16[4,32,2560]{2,1,0:T(8,128)(2,1)S(1)}, u32[]{:S(2)}) copy-start(bf16[4,32,2560]{2,1,0:T(8,128)(2,1)S(1)} %all-to-all-done) | copy-start | bytes 1966084
  25.6 2.2 %collective-permute-start.2 = (f32[1280,128]{1,0:T(8,128)S(1)}, f32[1280,128]{1,0:T(8,128)S(1)}, u32[]{:S(2)}, u32[]{:S(2)}) collective-permute-start(f32[1280,128]{1,0:T(8,128)S(1)} %get-tuple-element.16), channel_id=1, source_target_pairs={{0,1},{1,0},{2,3},{3,2},{4,5},{5,4},{6,7},{7,6},{8,9},{9,8},{10,11... | collective-permute-start | bytes 1966088 | tf_op jit(solution)/shard_map/basis/ppermute | solution.py:428
  27.8 62.4 %slice-start = ((s8[5079040]{0:T(1024)(128)(4,1)}), s8[884736]{0:T(1024)(128)(4,1)S(1)}, s32[]{:S(2)}) async-start(s8[5079040]{0:T(1024)(128)(4,1)} %bitcast.42), calls=%async_computation.7 | async-start | bytes 1769472
  65.7 24.4 %slice-start.1 = ((s8[5079040]{0:T(1024)(128)(4,1)}), s8[4194304]{0:T(1024)(128)(4,1)S(1)}, s32[]{:S(2)}) async-start(s8[5079040]{0:T(1024)(128)(4,1)} %bitcast.42), calls=%async_computation.8 | async-start | bytes 8388608
  80.8 2.1 %collective-permute-start.3 = (f32[1280,128]{1,0:T(8,128)S(1)}, f32[1280,128]{1,0:T(8,128)S(1)}, u32[]{:S(2)}, u32[]{:S(2)}) collective-permute-start(f32[1280,128]{1,0:T(8,128)S(1)} %bitcast.50), channel_id=1, source_target_pairs={{0,1},{1,0},{2,3},{3,2},{4,5},{5,4},{6,7},{7,6},{8,9},{9,8},{10,11... | collective-permute-start | bytes 1966088 | tf_op jit(solution)/shard_map/ppermute | solution.py:435
  80.8 9.3 %collective-permute-start = (bf16[128,2560]{1,0:T(8,128)(2,1)S(1)}, bf16[128,2560]{1,0:T(8,128)(2,1)S(1)}, u32[]{:S(2)}, u32[]{:S(2)}) collective-permute-start(bf16[128,2560]{1,0:T(8,128)(2,1)S(1)} %bitcast.46), channel_id=1, source_target_pairs={{0,1},{1,0},{2,3},{3,2},{4,5},{5,4},{6,7},{7,6},{8,9},{9,8},{10,11... | collective-permute-start | bytes 1966088 | tf_op jit(solution)/shard_map/gathers/ppermute | solution.py:423
  90.2 2.8 %copy-start.5 = (bf16[128,2560]{1,0:T(8,128)(2,1)}, bf16[128,2560]{1,0:T(8,128)(2,1)S(1)}, u32[]{:S(2)}) copy-start(bf16[128,2560]{1,0:T(8,128)(2,1)S(1)} %collective-permute-done.other_ref) | copy-start | bytes 1966084
  93.0 0.7 copy-start.3
  119.4 6.4 %collective-permute-start.4 = (f32[128,2560]{1,0:T(8,128)}, f32[128,2560]{1,0:T(8,128)}, u32[]{:S(2)}, u32[]{:S(2)}) collective-permute-start(f32[128,2560]{1,0:T(8,128)} %after.1), channel_id=1, source_target_pairs={{0,1},{1,0},{2,3},{3,2},{4,5},{5,4},{6,7},{7,6},{8,9},{9,8},{10,11... | collective-permute-start | bytes 3932168 | tf_op jit(solution)/shard_map/input_grad/ppermute | solution.py:445
  119.5 17.7 %all-to-all-start.5 = ((bf16[32,32,128]{2,1,0:T(8,128)(2,1)}), bf16[32,32,128]{2,1,0:T(8,128)(2,1)S(1)}, u32[]{:S(2)}, u32[]{:S(2)}) async-start(bf16[32,32,128]{2,1,0:T(8,128)(2,1)} %mean_copies.1.order_ref), calls=%async_computation.5 | async-start | bytes 524288 | tf_op jit(solution)/shard_map/right_factor/all_to_all | solution.py:441
  124.4 1.5 copy-start.7
  124.8 1.1 copy-start.4
  127.4 17.6 %collective-permute-start.5 = (bf16[32,2560]{1,0:T(8,128)(2,1)S(1)}, bf16[32,2560]{1,0:T(8,128)(2,1)S(1)}, u32[]{:S(2)}, u32[]{:S(2)}) collective-permute-start(bf16[32,2560]{1,0:T(8,128)(2,1)S(1)} %get-tuple-element.21), channel_id=1, source_target_pairs={{0,2},{1,3},{2,4},{3,5},{4,6},{5,7},{6,0},{7,1},{8,10},{9,11},{10,... | collective-permute-start | bytes 491528 | tf_op jit(solution)/shard_map/input_grad/ppermute | solution.py:410
  128.8 16.2 %collective-permute-start.7 = (bf16[32,2560]{1,0:T(8,128)(2,1)S(1)}, bf16[32,2560]{1,0:T(8,128)(2,1)S(1)}, u32[]{:S(2)}, u32[]{:S(2)}) collective-permute-start(bf16[32,2560]{1,0:T(8,128)(2,1)S(1)} %get-tuple-element.22), channel_id=1, source_target_pairs={{0,6},{1,7},{2,0},{3,1},{4,2},{5,3},{6,4},{7,5},{8,14},{9,15},{10,... | collective-permute-start | bytes 491528 | tf_op jit(solution)/shard_map/input_grad/ppermute | solution.py:410
  130.8 14.3 %collective-permute-start.6 = (bf16[32,2560]{1,0:T(8,128)(2,1)S(1)}, bf16[32,2560]{1,0:T(8,128)(2,1)S(1)}, u32[]{:S(2)}, u32[]{:S(2)}) collective-permute-start(bf16[32,2560]{1,0:T(8,128)(2,1)S(1)} %get-tuple-element.23), channel_id=1, source_target_pairs={{0,4},{1,5},{2,6},{3,7},{4,0},{5,1},{6,2},{7,3},{8,12},{9,13},{10,... | collective-permute-start | bytes 491528 | tf_op jit(solution)/shard_map/input_grad/ppermute | solution.py:410
  137.2 0.7 copy-start.10
Sparse Core Ops, SparseCore 0:
  10.6 97.4 all-gather.1
